TPU v7x, 512 devices: a whole 4x4x16 slice. The times are simulated.
512 devices in a mesh: pipe: 4 (over z_hi), dp: 16 (over y, x), tensor: 8 (over z_lo, core).
Axes of the slice: x: 4, y: 4, z: 16 (z_hi: 4, z_lo: 4; z = z_hi * 4 + z_lo), core: 2. Of those that a mesh axis runs over, the one named last changes fastest.
Arguments:
- x_in: bfloat16 [4, 2, 16, 128, 1600], P('pipe', None, 'dp', 'tensor'), may hold values from -6 to 6
- out_grad: bfloat16 [2, 16, 128, 1600], P(None, 'dp'), may hold values from -6 to 6
- layer_scale: float32 [4, 1600], P('pipe'), may hold values from 0.05 to 1
- norm_gain: float32 [4, 1600], P('pipe'), may hold values from 0.5 to 1.5
- master: float32 [4, 1600, 8192], P('pipe', 'dp', 'tensor'), may hold values from -0.15625 to 0.15625
- moment_one: float32 [4, 1600, 8192], P('pipe', 'dp', 'tensor'), may hold values from -4 to 4
- moment_two: float32 [4, 1600, 8192], P('pipe', 'dp', 'tensor'), may hold values from 0.05 to 5
Outputs:
- input_grads: bfloat16 [4, 2, 16, 128, 1600], P('pipe', None, 'dp', 'tensor')
- new_master: float32 [4, 1600, 8192], P('pipe', 'dp', 'tensor')
- new_moment_one: float32 [4, 1600, 8192], P('pipe', 'dp', 'tensor')
- new_moment_two: float32 [4, 1600, 8192], P('pipe', 'dp', 'tensor')
- scale_grads: float32 [4, 2, 1600], P('pipe')
All inputs are finite; a program needn't handle non-finite values.
Results may differ from a plain program's by a relative error of at most 0.027.
Values may be sent and summed in bfloat16 or wider, within the bound.
A program may use at most 128 MiB of HBM per device.

v0:
```python
import math

import jax
import jax.numpy as jnp
from jax import lax
from jax.sharding import PartitionSpec as P

HD = 128


beta_one = 0.9
beta_two = 0.95
adam_eps = 1e-08
learn_rate = 0.001
weight_decay = 0.05
adam_step = 100.0
norm_eps = 1e-06


def from_behind(block, axis, distance):
    devices = range(lax.axis_size(axis))
    route = [(i - distance, i) for i in devices if i - distance in devices]
    return lax.ppermute(block, axis, route)


def normalize(values_in):
    inverse = lax.rsqrt(jnp.mean(values_in * values_in, axis=-1, keepdims=True) + norm_eps)
    return (inverse, values_in * inverse)


def select_micro(array, micro_index):
    return lax.dynamic_index_in_dim(array, micro_index, 0, keepdims=False)


def store_slot(buffer, value, slot_index):
    return lax.dynamic_update_index_in_dim(buffer, value, slot_index, 0)


def local(x_in, out_grad, layer_scale, norm_gain, master, moment_one, moment_two):
    n_pipe = lax.axis_size("pipe")
    n_tensor = lax.axis_size("tensor")
    pipe_rank = lax.axis_index("pipe")
    micro_count = x_in.shape[1]
    images = x_in.shape[2]
    shard_len = x_in.shape[3]
    channels = x_in.shape[4]
    seq_len = shard_len * n_tensor
    row_start = lax.axis_index("tensor") * shard_len
    head_cols = master.shape[2] // 4
    local_heads = head_cols // HD
    score_root = math.sqrt(HD)
    scale_vec = layer_scale[0]
    gain_vec = norm_gain[0]
    weights = lax.all_gather(master[0].astype(jnp.bfloat16), "dp", axis=0, tiled=True)
    w_qkv = weights[:, : 3 * head_cols]
    w_out = weights[:, 3 * head_cols :]
    full_x = lax.all_gather(x_in[0], "tensor", axis=2, tiled=True).astype(jnp.float32)
    full_inverse, full_unit = normalize(full_x)
    normed = (full_unit * gain_vec).astype(jnp.bfloat16)
    local_unit = lax.dynamic_slice_in_dim(full_unit, row_start, shard_len, 2)
    projected = jnp.einsum(
        "mbsd,dc->mbsc", normed, w_qkv, preferred_element_type=jnp.float32
    ).astype(jnp.bfloat16)
    projected = projected.reshape(micro_count, images, seq_len, 3, local_heads, HD)
    query = projected[:, :, :, 0]
    keys = projected[:, :, :, 1]
    values = projected[:, :, :, 2]
    scores = (
        jnp.einsum("mbqhe,mbkhe->mbhqk", query, keys, preferred_element_type=jnp.float32)
        / score_root
    )
    probs = jax.nn.softmax(scores, axis=-1)
    probs_low = probs.astype(jnp.bfloat16)
    attended = jnp.einsum(
        "mbhqk,mbkhe->mbqhe", probs_low, values, preferred_element_type=jnp.float32
    ).astype(jnp.bfloat16)
    attended_flat = attended.reshape(micro_count, images, seq_len, head_cols)

    def backward_segment(micro_index, incoming):
        query_now = select_micro(query, micro_index)
        keys_now = select_micro(keys, micro_index)
        values_now = select_micro(values, micro_index)
        probs_now = select_micro(probs, micro_index)
        probs_low_now = select_micro(probs_low, micro_index)
        attended_now = select_micro(attended, micro_index)
        scaled = (scale_vec * incoming.astype(jnp.float32)).astype(jnp.bfloat16)
        d_att = jnp.einsum("bsd,dc->bsc", scaled, w_out, preferred_element_type=jnp.float32).astype(
            jnp.bfloat16
        )
        d_att = d_att.reshape(images, seq_len, local_heads, HD)
        d_prob = jnp.einsum(
            "bqhe,bkhe->bhqk", d_att, values_now, preferred_element_type=jnp.float32
        )
        row_delta = jnp.einsum(
            "bqhe,bqhe->bhq", d_att, attended_now, preferred_element_type=jnp.float32
        )
        d_score = (probs_now * (d_prob - row_delta[..., None]) / score_root).astype(jnp.bfloat16)
        d_query = jnp.einsum(
            "bhqk,bkhe->bqhe", d_score, keys_now, preferred_element_type=jnp.float32
        ).astype(jnp.bfloat16)
        d_keys = jnp.einsum(
            "bhqk,bqhe->bkhe", d_score, query_now, preferred_element_type=jnp.float32
        ).astype(jnp.bfloat16)
        d_values = jnp.einsum(
            "bhqk,bqhe->bkhe", probs_low_now, d_att, preferred_element_type=jnp.float32
        ).astype(jnp.bfloat16)
        d_proj = jnp.concatenate([d_query, d_keys, d_values], axis=2).reshape(
            images, seq_len, 3 * head_cols
        )
        partial_sum = jnp.einsum("bsc,dc->bsd", d_proj, w_qkv, preferred_element_type=jnp.float32)
        return (partial_sum, d_proj, scaled)

    def spare_segment(micro_index, incoming):
        return (
            jnp.zeros((images, seq_len, channels), jnp.float32),
            jnp.zeros((images, seq_len, 3 * head_cols), jnp.bfloat16),
            jnp.zeros((images, seq_len, channels), jnp.bfloat16),
        )

    segments = n_pipe + micro_count - 1
    is_last = pipe_rank == n_pipe - 1
    received = jnp.zeros((images, seq_len, channels), jnp.bfloat16)
    slots = micro_count + 1
    grads_out = jnp.zeros((slots, images, shard_len, channels), jnp.bfloat16)
    proj_saved = jnp.zeros((slots, images, seq_len, 3 * head_cols), jnp.bfloat16)
    scaled_saved = jnp.zeros((slots, images, seq_len, channels), jnp.bfloat16)
    grad_saved = jnp.zeros((slots, images, seq_len, channels), jnp.bfloat16)
    gain_part = jnp.zeros((channels,), jnp.float32)
    for segment_step in range(segments):
        micro_index = segment_step - (n_pipe - 1) + pipe_rank
        active = jnp.logical_and(micro_index >= 0, micro_index < micro_count)
        micro_index = jnp.clip(micro_index, 0, micro_count - 1)
        slot_index = jnp.where(active, micro_index, micro_count)
        arrived = received
        incoming = jnp.where(is_last, select_micro(out_grad, micro_index), arrived)
        partial_sum, d_proj, scaled = lax.cond(
            active, backward_segment, spare_segment, micro_index, incoming
        )
        pieces = partial_sum.astype(jnp.bfloat16).reshape(images, n_tensor, shard_len, channels)
        landed = lax.all_to_all(pieces, "tensor", split_axis=1, concat_axis=1, tiled=True)
        own_d = jnp.sum(landed.astype(jnp.float32), axis=1)
        d_normed = lax.all_gather(own_d.astype(jnp.bfloat16), "tensor", axis=1, tiled=True).astype(
            own_d.dtype
        )
        own_unit = select_micro(local_unit, micro_index)
        sel_unit = select_micro(full_unit, micro_index)
        sel_inverse = select_micro(full_inverse, micro_index)
        d_unit = d_normed * gain_vec
        d_input = sel_inverse * (
            d_unit - sel_unit * jnp.mean(d_unit * sel_unit, axis=-1, keepdims=True)
        )
        passed = (incoming.astype(jnp.float32) + d_input).astype(jnp.bfloat16)
        own_passed = lax.dynamic_slice_in_dim(passed, row_start, shard_len, 1)
        gain_part = gain_part + jnp.where(active, jnp.sum(own_d * own_unit, axis=(0, 1)), 0.0)
        grads_out = store_slot(grads_out, own_passed, slot_index)
        proj_saved = store_slot(proj_saved, d_proj, slot_index)
        scaled_saved = store_slot(scaled_saved, scaled, slot_index)
        grad_saved = store_slot(grad_saved, incoming, slot_index)
        if segment_step + 1 < segments:
            received = from_behind(passed, "pipe", -1)
    grads_kept = grads_out[:micro_count]
    proj_kept = proj_saved[:micro_count]
    scaled_kept = scaled_saved[:micro_count]
    grad_kept = grad_saved[:micro_count]
    grad_qkv = jnp.einsum("mbsd,mbsc->dc", normed, proj_kept, preferred_element_type=jnp.float32)
    grad_out = jnp.einsum(
        "mbsd,mbsc->dc", scaled_kept, attended_flat, preferred_element_type=jnp.float32
    )
    weight_grad = lax.psum_scatter(
        jnp.concatenate([grad_qkv, grad_out], axis=1).astype(jnp.bfloat16),
        "dp",
        scatter_dimension=0,
        tiled=True,
    ).astype(jnp.float32)
    summed_out = jnp.einsum(
        "mbsd,mbsc->dc", grad_kept, attended_flat, preferred_element_type=jnp.float32
    )
    scale_part = jnp.sum(w_out.astype(jnp.float32) * summed_out, axis=1)
    scale_grad, gain_grad = lax.psum((scale_part, gain_part), ("dp", "tensor"))
    bias_one = 1.0 - beta_one**adam_step
    bias_two = 1.0 - beta_two**adam_step
    first_new = beta_one * moment_one[0] + (1.0 - beta_one) * weight_grad
    second_new = beta_two * moment_two[0] + (1.0 - beta_two) * weight_grad * weight_grad
    update = first_new / bias_one / (jnp.sqrt(second_new / bias_two) + adam_eps)
    master_new = master[0] - learn_rate * (update + weight_decay * master[0])
    scale_both = jnp.stack([scale_grad, gain_grad])
    return (grads_kept[None], master_new[None], first_new[None], second_new[None], scale_both[None])


def solution(mesh):
    placed = (
        P("pipe", None, "dp", "tensor", None),
        P(None, "dp", None, None),
        P("pipe", None),
        P("pipe", None),
        P("pipe", "dp", "tensor"),
        P("pipe", "dp", "tensor"),
        P("pipe", "dp", "tensor"),
    )
    return jax.shard_map(
        local,
        mesh=mesh,
        in_specs=placed,
        out_specs=(
            P("pipe", None, "dp", "tensor", None),
            P("pipe", "dp", "tensor"),
            P("pipe", "dp", "tensor"),
            P("pipe", "dp", "tensor"),
            P("pipe", None, None),
        ),
        check_vma=False,
    )
```

profile of v0, /device:TPU:1, one launch (start us, length us, event | category | flops | bytes accessed | tf_op | source)
XLA Modules:
  0.0 1391.1 jit_solution(9497189529222593364)
XLA Ops:
  9.8 22.7 %all-gather = bf16[1,2,1,128,1600]{4,3,2,1,0:T(8,128)(2,1)S(1)} all-gather(bf16[1,2,1,16,1600]{4,3,2,1,0:T(8,128)(2,1)} %param.17), channel_id=2, replica_groups=mesh['pipe'=4,'dp'=16,'tensor'=8] {'tensor'}, dimensions={3}, use_global_device_ids=true | all-gather | bytes 921600 | tf_op jit(solution)/shard_map/all_gather | solution.py:57
  33.6 47.1 %all-gather.9.cloned.1.call-done = bf16[16,100,1024]{2,1,0:T(8,128)(2,1)} async-done(((bf16[1,100,1024]{2,1,0:T(8,128)(2,1)}), bf16[16,100,1024]{2,1,0:T(8,128)(2,1)}) %all-gather.9.cloned.1.call-update) | async-done | bytes 3276816 | tf_op jit(solution)/shard_map/all_gather | solution.py:54
  80.7 2.9 reshape.819
  83.7 3.4 fusion.113
  104.4 5.8 all-to-all-start
  114.3 2.4 copy.217
  118.1 4.7 all-to-all-done
  124.5 16.3 %all-gather.1 = bf16[128,1600]{1,0:T(8,128)(2,1)} all-gather(bf16[16,1600]{1,0:T(8,128)(2,1)S(1)} %convert_element_type.421), channel_id=3, replica_groups=mesh['pipe'=4,'dp'=16,'tensor'=8] {'tensor'}, dimensions={0}, use_global_device_ids=true | all-gather | bytes 460800 | tf_op jit(solution)/shard_map/all_gather | solution.py:142
  149.2 40.3 %collective-permute-done = bf16[1,128,1600]{1,2,0:T(8,128)(2,1)} collective-permute-done((bf16[1,128,1600]{1,2,0:T(8,128)(2,1)}, bf16[1,128,1600]{1,2,0:T(8,128)(2,1)}, u32[]{:S(2)}, u32[]{:S(2)}) %collective-permute-start) | collective-permute-done | bytes 409632 | tf_op jit(solution)/shard_map/ppermute | solution.py:23
  192.5 2.5 conditional.6
  196.9 4.4 all-to-all-start.1
  201.3 2.4 copy.231
  203.7 10.2 all-to-all-done.1
  215.6 16.3 %all-gather.2 = bf16[128,1600]{1,0:T(8,128)(2,1)} all-gather(bf16[16,1600]{1,0:T(8,128)(2,1)S(1)} %convert_element_type.429), channel_id=4, replica_groups=mesh['pipe'=4,'dp'=16,'tensor'=8] {'tensor'}, dimensions={0}, use_global_device_ids=true | all-gather | bytes 460800 | tf_op jit(solution)/shard_map/all_gather | solution.py:142
  239.0 41.4 %collective-permute-done.1 = bf16[1,128,1600]{1,2,0:T(8,128)(2,1)} collective-permute-done((bf16[1,128,1600]{1,2,0:T(8,128)(2,1)}, bf16[1,128,1600]{1,2,0:T(8,128)(2,1)}, u32[]{:S(2)}, u32[]{:S(2)}) %collective-permute-start.1) | collective-permute-done | bytes 409632 | tf_op jit(solution)/shard_map/ppermute | solution.py:23
  282.6 2.3 conditional.7
  286.9 4.4 all-to-all-start.2
  291.3 2.3 copy.245
  293.7 2.3 copy.259
  296.0 2.4 copy.273
  312.5 16.0 %all-gather.3 = bf16[128,1600]{1,0:T(8,128)(2,1)} all-gather(bf16[16,1600]{1,0:T(8,128)(2,1)S(1)} %convert_element_type.437), channel_id=5, replica_groups=mesh['pipe'=4,'dp'=16,'tensor'=8] {'tensor'}, dimensions={0}, use_global_device_ids=true | all-gather | bytes 460800 | tf_op jit(solution)/shard_map/all_gather | solution.py:142
  338.4 127.8 %collective-permute-done.2 = bf16[1,128,1600]{1,2,0:T(8,128)(2,1)S(1)} collective-permute-done((bf16[1,128,1600]{1,2,0:T(8,128)(2,1)S(1)}, bf16[1,128,1600]{1,2,0:T(8,128)(2,1)S(1)}, u32[]{:S(2)}, u32[]{:S(2)}) %collective-permute-start.2) | collective-permute-done | bytes 409632 | tf_op jit(solution)/shard_map/ppermute | solution.py:23
  467.2 34.3 %conditional.8 = (bf16[1,128,1600]{1,2,0:T(8,128)(2,1)}, bf16[1,1,128,768]{3,2,0,1:T(8,128)(2,1)}, bf16[1,1,128,1600]{2,3,0,1:T(8,128)(2,1)}) conditional(s32[]{:T(128)} %convert_element_type.442, () %tuple.74, (s32[]{:T(128)}, bf16[2,1,128,2,128]{4,2,3,0,1:T(8,128)(2,1)}, f32[2,1,2,128,128]{3,4,2,0,1:T(8,128)S(1)}, f32[1,1600]{1,0:T(1,128)S(1)}, ...), branch_computations={%region_15.16_spmd, %region_16.17_spmd} | conditional | flops 454803200 | bytes 11565162 | solution.py:136
  503.4 4.5 all-to-all-start.3
  526.9 16.0 %all-gather.4 = bf16[128,1600]{1,0:T(8,128)(2,1)} all-gather(bf16[16,1600]{1,0:T(8,128)(2,1)S(1)} %convert_element_type.445), channel_id=6, replica_groups=mesh['pipe'=4,'dp'=16,'tensor'=8] {'tensor'}, dimensions={0}, use_global_device_ids=true | all-gather | bytes 460800 | tf_op jit(solution)/shard_map/all_gather | solution.py:142
  555.0 16.3 %collective-permute-done.3 = bf16[1,128,1600]{1,2,0:T(8,128)(2,1)} collective-permute-done((bf16[1,128,1600]{1,2,0:T(8,128)(2,1)}, bf16[1,128,1600]{1,2,0:T(8,128)(2,1)}, u32[]{:S(2)}, u32[]{:S(2)}) %collective-permute-start.3) | collective-permute-done | bytes 409632 | tf_op jit(solution)/shard_map/ppermute | solution.py:23
  573.5 13.4 conditional.9
  589.0 25.6 %all-to-all-start.4 = ((bf16[1,8,16,1600]{3,2,0,1:T(8,128)(2,1)}), bf16[1,8,16,1600]{3,2,0,1:T(8,128)(2,1)}, u32[]{:S(2)}, u32[]{:S(2)}) async-start(bf16[1,8,16,1600]{3,2,0,1:T(8,128)(2,1)} %bitcast.151), calls=%async_computation.4 | async-start | bytes 851968 | tf_op jit(solution)/shard_map/all_to_all | solution.py:140
  622.0 61.9 %fusion = bf16[112,1024]{1,0:T(8,128)(2,1)} fusion(bf16[1600,1024]{1,0:T(8,128)(2,1)S(1)} %pad_maximum_fusion.5), kind=kCustom, calls=%all-reduce-scatter | all-reduce-scatter fusion | flops 1835009 | bytes 3508224
  686.7 3.7 collective-permute-start.5
  700.4 20.2 %all-gather.5 = bf16[128,1600]{1,0:T(8,128)(2,1)S(1)} all-gather(bf16[16,1600]{1,0:T(8,128)(2,1)S(1)} %get-tuple-element.430), channel_id=7, replica_groups=mesh['pipe'=4,'dp'=16,'tensor'=8] {'tensor'}, dimensions={0}, use_global_device_ids=true | all-gather | bytes 460800 | tf_op jit(solution)/shard_map/all_gather | solution.py:142
  722.7 660.5 %all-reduce.2 = (f32[1,1600]{1,0:T(1,128)S(1)}, f32[1,1600]{1,0:T(1,128)S(1)}) all-reduce(f32[1,1600]{1,0:T(1,128)S(1)} %stack.10, f32[1,1600]{1,0:T(1,128)S(1)} %stack.9), channel_id=1, replica_groups=mesh['pipe'=4,'dp'=16,'tensor'=8] {'dp','tensor'}, use_global_device_ids=true, to_apply=%region_31.32 | all-reduce | flops 3200 | bytes 25600 | tf_op jit(solution)/shard_map/psum | solution.py:179
  (257 shorter events, 192.9 us)
Async XLA Ops:
  7.2 25.6 %copy-start.2 = (bf16[2,1,128,1600]{2,3,1,0:T(8,128)(2,1)S(1)}, bf16[2,1,128,1600]{2,3,1,0:T(8,128)(2,1)}, u32[]{:S(2)}) copy-start(bf16[2,1,128,1600]{2,3,1,0:T(8,128)(2,1)} %param.18) | copy-start | bytes 2457604
  7.2 73.5 %all-gather.9.cloned.1.call-start = ((), (), s32[]{:S(2)}) async-start(), calls=%async_computation.5 | async-start | bytes 3620864 | tf_op jit(solution)/shard_map/all_gather | solution.py:54
  32.8 50.9 %copy-start.44 = (f32[2,128]{1,0:T(2,128)}, f32[2,128]{1,0:T(2,128)S(1)}, u32[]{:S(2)}) copy-start(f32[2,128]{1,0:T(2,128)S(1)} %add_rsqrt_fusion) | copy-start | bytes 3076
  90.3 5.4 copy-start.34
  95.7 4.5 copy-start.42
  104.4 18.3 %all-to-all-start = ((bf16[1,8,16,1600]{3,2,0,1:T(8,128)(2,1)}), bf16[1,8,16,1600]{3,2,0,1:T(8,128)(2,1)}, u32[]{:S(2)}, u32[]{:S(2)}) async-start(bf16[1,8,16,1600]{3,2,0,1:T(8,128)(2,1)} %bitcast.535), calls=%async_computation | async-start | bytes 851968 | tf_op jit(solution)/shard_map/all_to_all | solution.py:140
  146.5 42.9 %collective-permute-start = (bf16[1,128,1600]{1,2,0:T(8,128)(2,1)}, bf16[1,128,1600]{1,2,0:T(8,128)(2,1)}, u32[]{:S(2)}, u32[]{:S(2)}) collective-permute-start(bf16[1,128,1600]{1,2,0:T(8,128)(2,1)} %fusion.145), channel_id=1, source_target_pairs={{128,0},{256,128},{384,256},{129,1},{257,129},{385,257},{130,2},{2... | collective-permute-start | bytes 1228808 | tf_op jit(solution)/shard_map/ppermute | solution.py:23
  147.9 41.6 %copy-start.3 = (bf16[2,1,128,1600]{2,3,1,0:T(8,128)(2,1)S(1)}, bf16[2,1,128,1600]{2,3,1,0:T(8,128)(2,1)}, u32[]{:S(2)}) copy-start(bf16[2,1,128,1600]{2,3,1,0:T(8,128)(2,1)} %param.18) | copy-start | bytes 2457604
  196.9 16.9 %all-to-all-start.1 = ((bf16[1,8,16,1600]{3,2,0,1:T(8,128)(2,1)}), bf16[1,8,16,1600]{3,2,0,1:T(8,128)(2,1)}, u32[]{:S(2)}, u32[]{:S(2)}) async-start(bf16[1,8,16,1600]{3,2,0,1:T(8,128)(2,1)} %bitcast.537), calls=%async_computation.1 | async-start | bytes 851968 | tf_op jit(solution)/shard_map/all_to_all | solution.py:140
  237.7 42.7 %collective-permute-start.1 = (bf16[1,128,1600]{1,2,0:T(8,128)(2,1)}, bf16[1,128,1600]{1,2,0:T(8,128)(2,1)}, u32[]{:S(2)}, u32[]{:S(2)}) collective-permute-start(bf16[1,128,1600]{1,2,0:T(8,128)(2,1)} %fusion.139), channel_id=1, source_target_pairs={{128,0},{256,128},{384,256},{129,1},{257,129},{385,257},{130,2},{2... | collective-permute-start | bytes 1228808 | tf_op jit(solution)/shard_map/ppermute | solution.py:23
  286.9 23.8 %all-to-all-start.2 = ((bf16[1,8,16,1600]{3,2,0,1:T(8,128)(2,1)}), bf16[1,8,16,1600]{3,2,0,1:T(8,128)(2,1)}, u32[]{:S(2)}, u32[]{:S(2)}) async-start(bf16[1,8,16,1600]{3,2,0,1:T(8,128)(2,1)} %bitcast.534), calls=%async_computation.2 | async-start | bytes 851968 | tf_op jit(solution)/shard_map/all_to_all | solution.py:140
  332.0 134.1 %copy-start.4 = (bf16[2,1,128,1600]{2,3,1,0:T(8,128)(2,1)S(1)}, bf16[2,1,128,1600]{2,3,1,0:T(8,128)(2,1)}, u32[]{:S(2)}) copy-start(bf16[2,1,128,1600]{2,3,1,0:T(8,128)(2,1)} %param.18) | copy-start | bytes 2457604
  333.5 133.6 %copy-start.22 = (bf16[1,128,1600]{1,2,0:T(8,128)(2,1)}, bf16[1,128,1600]{1,2,0:T(8,128)(2,1)S(1)}, u32[]{:S(2)}) copy-start(bf16[1,128,1600]{1,2,0:T(8,128)(2,1)S(1)} %fusion.133) | copy-start | bytes 1228804
  333.5 132.6 %collective-permute-start.2 = (bf16[1,128,1600]{1,2,0:T(8,128)(2,1)S(1)}, bf16[1,128,1600]{1,2,0:T(8,128)(2,1)S(1)}, u32[]{:S(2)}, u32[]{:S(2)}) collective-permute-start(bf16[1,128,1600]{1,2,0:T(8,128)(2,1)S(1)} %fusion.133), channel_id=1, source_target_pairs={{128,0},{256,128},{384,256},{129,1},{257,129},{385,257},{130,2},{2... | collective-permute-start | bytes 1228808 | tf_op jit(solution)/shard_map/ppermute | solution.py:23
  334.9 132.3 %copy-start.36 = (bf16[3,1,16,1600]{3,2,0,1:T(8,128)(2,1)}, bf16[3,1,16,1600]{3,2,0,1:T(8,128)(2,1)S(1)}, u32[]{:S(2)}) copy-start(bf16[3,1,16,1600]{3,2,0,1:T(8,128)(2,1)S(1)} %constant_dynamic-update-slice_fusion.14) | copy-start | bytes 460804
  503.4 21.7 %all-to-all-start.3 = ((bf16[1,8,16,1600]{3,2,0,1:T(8,128)(2,1)}), bf16[1,8,16,1600]{3,2,0,1:T(8,128)(2,1)}, u32[]{:S(2)}, u32[]{:S(2)}) async-start(bf16[1,8,16,1600]{3,2,0,1:T(8,128)(2,1)} %bitcast.536), calls=%async_computation.3 | async-start | bytes 851968 | tf_op jit(solution)/shard_map/all_to_all | solution.py:140
  548.6 22.8 %collective-permute-start.3 = (bf16[1,128,1600]{1,2,0:T(8,128)(2,1)}, bf16[1,128,1600]{1,2,0:T(8,128)(2,1)}, u32[]{:S(2)}, u32[]{:S(2)}) collective-permute-start(bf16[1,128,1600]{1,2,0:T(8,128)(2,1)} %fusion.127), channel_id=1, source_target_pairs={{128,0},{256,128},{384,256},{129,1},{257,129},{385,257},{130,2},{2... | collective-permute-start | bytes 1228808 | tf_op jit(solution)/shard_map/ppermute | solution.py:23
  578.1 4.8 copy-start.14
  578.1 5.1 copy-start.15
  586.9 29.3 %copy-start.6 = (bf16[1,2,1,128,1600]{4,3,2,1,0:T(8,128)(2,1)S(1)}, bf16[1,2,1,128,1600]{4,3,2,1,0:T(8,128)(2,1)}, u32[]{:S(2)}) copy-start(bf16[1,2,1,128,1600]{4,3,2,1,0:T(8,128)(2,1)} %copy-done.5) | copy-start | bytes 2457604
  586.9 29.3 %copy-start.45 = (f32[2,128]{1,0:T(2,128)S(1)}, f32[2,128]{1,0:T(2,128)}, u32[]{:S(2)}) copy-start(f32[2,128]{1,0:T(2,128)} %copy-done.44) | copy-start | bytes 3076
  589.0 108.8 %all-to-all-start.4 = ((bf16[1,8,16,1600]{3,2,0,1:T(8,128)(2,1)}), bf16[1,8,16,1600]{3,2,0,1:T(8,128)(2,1)}, u32[]{:S(2)}, u32[]{:S(2)}) async-start(bf16[1,8,16,1600]{3,2,0,1:T(8,128)(2,1)} %bitcast.151), calls=%async_computation.4 | async-start | bytes 851968 | tf_op jit(solution)/shard_map/all_to_all | solution.py:140
  683.9 9.2 copy-start.24
  684.9 8.2 collective-permute-start.4
  686.7 6.3 collective-permute-start.5
  694.2 4.7 copy-start.27
  694.2 4.7 copy-start.29
  694.2 4.7 copy-start.31
  694.2 4.7 copy-start.33
  697.8 23.0 %copy-start.10 = (f32[1,1,128,1600]{2,3,1,0:T(8,128)S(1)}, f32[1,1,128,1600]{2,3,1,0:T(8,128)}, u32[]{:S(2)}) copy-start(f32[1,1,128,1600]{2,3,1,0:T(8,128)} %copy.273) | copy-start | bytes 2457604
  700.4 20.8 %copy-start.17 = (bf16[1,128,1600]{1,2,0:T(8,128)(2,1)S(1)}, bf16[1,128,1600]{1,2,0:T(8,128)(2,1)}, u32[]{:S(2)}) copy-start(bf16[1,128,1600]{1,2,0:T(8,128)(2,1)} %get-tuple-element.408) | copy-start | bytes 1228804
  700.4 20.8 %copy-start.46 = (f32[16]{0:T(128)S(1)}, f32[16]{0:T(128)}, u32[]{:S(2)}) copy-start(f32[16]{0:T(128)} %dynamic-slice.8) | copy-start | bytes 196
  (24 other events, 50.4 us)
Sparse Core Ops, SparseCore 0:
  11.6 69.0 all-gather.8
where the time goes:
time: 1410 us; the launch traced here: 1390 us
  blocking collectives  830 us (59%)
  waiting for transfers between devices  288 us (20%)
  local copies, waits for them, and re-layouts  131 us (9%)
  starting transfers between devices  55.6 us (4%)
  other arithmetic  43 us (3%)
  matrix products  27.1 us (2%)
  between operations  15.8 us (1%)
    psum x1, blocking collectives, local(): scale_grad, gain_grad = lax.psum((scale_part, gain_part), ('dp', 'tensor'))  660 us
    ppermute x4, waiting for transfers between devices, from_behind(): return lax.ppermute(block, axis, route)  226 us
    all_gather x5, blocking collectives, local(): lax.all_gather(own_d.astype(jnp.bfloat16), 'tensor', axis=1, tiled=True)  84.6 us
    unnamed x1, blocking collectives  61.9 us
    all_gather x1, waiting for transfers between devices, local(): lax.all_gather(master[0].astype(jnp.bfloat16), 'dp', axis=0, tiled=True)  47.1 us
    all_to_all x5, starting transfers between devices, local(): lax.all_to_all(pieces, 'tensor', split_axis=1, concat_axis=1, tiled=True)  44.9 us
  transfers between devices with their start and end apart: 12, of which 8 were waited for; matrix products, arithmetic and copies ran while one was open for 10% of the time, Pallas kernels for 0%

commit v1 on v0

--- a/solution.py
+++ b/solution.py
@@ -58,6 +58,7 @@
     full_inverse, full_unit = normalize(full_x)
     normed = (full_unit * gain_vec).astype(jnp.bfloat16)
     local_unit = lax.dynamic_slice_in_dim(full_unit, row_start, shard_len, 2)
+    local_inverse = lax.dynamic_slice_in_dim(full_inverse, row_start, shard_len, 2)
     projected = jnp.einsum(
         "mbsd,dc->mbsc", normed, w_qkv, preferred_element_type=jnp.float32
     ).astype(jnp.bfloat16)
@@ -139,25 +140,22 @@
         pieces = partial_sum.astype(jnp.bfloat16).reshape(images, n_tensor, shard_len, channels)
         landed = lax.all_to_all(pieces, "tensor", split_axis=1, concat_axis=1, tiled=True)
         own_d = jnp.sum(landed.astype(jnp.float32), axis=1)
-        d_normed = lax.all_gather(own_d.astype(jnp.bfloat16), "tensor", axis=1, tiled=True).astype(
-            own_d.dtype
-        )
         own_unit = select_micro(local_unit, micro_index)
-        sel_unit = select_micro(full_unit, micro_index)
-        sel_inverse = select_micro(full_inverse, micro_index)
-        d_unit = d_normed * gain_vec
-        d_input = sel_inverse * (
-            d_unit - sel_unit * jnp.mean(d_unit * sel_unit, axis=-1, keepdims=True)
-        )
-        passed = (incoming.astype(jnp.float32) + d_input).astype(jnp.bfloat16)
-        own_passed = lax.dynamic_slice_in_dim(passed, row_start, shard_len, 1)
+        own_inverse = select_micro(local_inverse, micro_index)
+        d_unit = own_d * gain_vec
+        d_input = own_inverse * (
+            d_unit - own_unit * jnp.mean(d_unit * own_unit, axis=-1, keepdims=True)
+        )
+        own_incoming = lax.dynamic_slice_in_dim(incoming, row_start, shard_len, 1)
+        own_passed = (own_incoming.astype(jnp.float32) + d_input).astype(jnp.bfloat16)
         gain_part = gain_part + jnp.where(active, jnp.sum(own_d * own_unit, axis=(0, 1)), 0.0)
         grads_out = store_slot(grads_out, own_passed, slot_index)
         proj_saved = store_slot(proj_saved, d_proj, slot_index)
         scaled_saved = store_slot(scaled_saved, scaled, slot_index)
         grad_saved = store_slot(grad_saved, incoming, slot_index)
         if segment_step + 1 < segments:
-            received = from_behind(passed, "pipe", -1)
+            moved = from_behind(own_passed, "pipe", -1)
+            received = lax.all_gather(moved, "tensor", axis=1, tiled=True)
     grads_kept = grads_out[:micro_count]
     proj_kept = proj_saved[:micro_count]
     scaled_kept = scaled_saved[:micro_count]
@@ -176,14 +174,13 @@
         "mbsd,mbsc->dc", grad_kept, attended_flat, preferred_element_type=jnp.float32
     )
     scale_part = jnp.sum(w_out.astype(jnp.float32) * summed_out, axis=1)
-    scale_grad, gain_grad = lax.psum((scale_part, gain_part), ("dp", "tensor"))
+    scale_both = lax.psum(lax.psum(jnp.stack([scale_part, gain_part]), "tensor"), "dp")
     bias_one = 1.0 - beta_one**adam_step
     bias_two = 1.0 - beta_two**adam_step
     first_new = beta_one * moment_one[0] + (1.0 - beta_one) * weight_grad
     second_new = beta_two * moment_two[0] + (1.0 - beta_two) * weight_grad * weight_grad
     update = first_new / bias_one / (jnp.sqrt(second_new / bias_two) + adam_eps)
     master_new = master[0] - learn_rate * (update + weight_decay * master[0])
-    scale_both = jnp.stack([scale_grad, gain_grad])
     return (grads_kept[None], master_new[None], first_new[None], second_new[None], scale_both[None])
 
 

time: 1410 us -> 842 us (0.60)
  the two profiles are of different devices: /device:TPU:1 before, /device:TPU:128 now
where the time goes in v1:
time: 842 us; the launch traced here: 831 us
  blocking collectives  302 us (36%)
  waiting for transfers between devices  252 us (30%)
  local copies, waits for them, and re-layouts  145 us (17%)
  other arithmetic  54.5 us (6%)
  starting transfers between devices  34.3 us (4%)
  matrix products  27.2 us (3%)
  between operations  15.5 us (2%)
    ppermute x4, waiting for transfers between devices, from_behind(): return lax.ppermute(block, axis, route)  187 us
    unnamed x1, blocking collectives  85 us
    all_gather x4, blocking collectives, local(): received = lax.all_gather(moved, 'tensor', axis=1, tiled=True)  84.8 us
    psum x1, blocking collectives, local(): lax.psum(lax.psum(jnp.stack([scale_part, gain_part]), 'tensor'), 'dp')  71.2 us
    all_gather x1, waiting for transfers between devices, local(): lax.all_gather(master[0].astype(jnp.bfloat16), 'dp', axis=0, tiled=True)  50.3 us
    another operation x23, local copies, waits for them, and re-layouts  32.2 us
    psum x1, blocking collectives, local(): lax.psum(jnp.stack([scale_part, gain_part]), 'tensor')  27 us
    dynamic_update_slice x15, local copies, waits for them, and re-layouts, store_slot(): return lax.dynamic_update_index_in_dim(buffer, value, slot_index, 0)  22.6 us
  transfers between devices with their start and end apart: 11, of which 8 were waited for; matrix products, arithmetic and copies ran while one was open for 16% of the time, Pallas kernels for 0%

profile of v1, /device:TPU:128, one launch (start us, length us, event | category | flops | bytes accessed | tf_op | source)
XLA Modules:
  0.0 831.2 jit_solution(14182584001447104835)
XLA Ops:
  9.8 17.2 %all-gather = bf16[1,2,1,128,1600]{4,3,2,1,0:T(8,128)(2,1)S(1)} all-gather(bf16[1,2,1,16,1600]{4,3,2,1,0:T(8,128)(2,1)} %param.17), channel_id=2, replica_groups=mesh['pipe'=4,'dp'=16,'tensor'=8] {'tensor'}, dimensions={3}, use_global_device_ids=true | all-gather | bytes 921600 | tf_op jit(solution)/shard_map/all_gather | solution.py:57
  28.4 50.3 %all-gather.4.cloned.1.call-done = bf16[16,100,1024]{2,1,0:T(8,128)(2,1)} async-done(((bf16[1,100,1024]{2,1,0:T(8,128)(2,1)}), bf16[16,100,1024]{2,1,0:T(8,128)(2,1)}) %all-gather.4.cloned.1.call-update) | async-done | bytes 3276816 | tf_op jit(solution)/shard_map/all_gather | solution.py:54
  78.8 4.5 reshape.1362
  84.5 2.6 fusion.115
  95.5 2.3 conditional.5
  99.8 4.8 all-to-all-start
  106.1 2.5 convert_multiply_fusion.6
  108.6 9.3 %all-to-all-done = bf16[1,8,16,1600]{3,2,0,1:T(8,128)(2,1)} async-done(((bf16[1,8,16,1600]{3,2,0,1:T(8,128)(2,1)}), bf16[1,8,16,1600]{3,2,0,1:T(8,128)(2,1)}, u32[]{:S(2)}, u32[]{:S(2)}) %all-to-all-start) | async-done | bytes 409632 | tf_op jit(solution)/shard_map/all_to_all | solution.py:141
  121.8 2.2 fusion.165
  132.2 40.1 %collective-permute-done = bf16[1,16,1600]{1,2,0:T(8,128)(2,1)} collective-permute-done((bf16[1,16,1600]{1,2,0:T(8,128)(2,1)}, bf16[1,16,1600]{1,2,0:T(8,128)(2,1)}, u32[]{:S(2)}, u32[]{:S(2)}) %collective-permute-start) | collective-permute-done | bytes 51232 | tf_op jit(solution)/shard_map/ppermute | solution.py:23
  174.1 15.8 %all_gather.20 = bf16[1,128,1600]{2,1,0:T(8,128)(2,1)} all-gather(bf16[1,16,1600]{2,1,0:T(8,128)(2,1)} %copy.219), channel_id=1, replica_groups=mesh['pipe'=4,'dp'=16,'tensor'=8] {'tensor'}, dimensions={1}, use_global_device_ids=true | all-gather | bytes 460800 | tf_op jit(solution)/shard_map/all_gather | solution.py:158
  194.0 2.7 conditional.6
  198.7 16.6 %all_to_all.25 = bf16[1,8,16,1600]{3,2,0,1:T(8,128)(2,1)S(1)} all-to-all(bf16[1,8,16,1600]{3,2,0,1:T(8,128)(2,1)} %bitcast.592), channel_id=1, replica_groups=mesh['pipe'=4,'dp'=16,'tensor'=8] {'tensor'}, dimensions={1} | all-to-all | bytes 819200 | tf_op jit(solution)/shard_map/all_to_all | solution.py:141
  228.6 94.0 %collective-permute-done.1 = bf16[1,16,1600]{1,2,0:T(8,128)(2,1)} collective-permute-done((bf16[1,16,1600]{1,2,0:T(8,128)(2,1)}, bf16[1,16,1600]{1,2,0:T(8,128)(2,1)}, u32[]{:S(2)}, u32[]{:S(2)}) %collective-permute-start.1) | collective-permute-done | bytes 51232 | tf_op jit(solution)/shard_map/ppermute | solution.py:23
  324.4 15.8 %all_gather.21 = bf16[1,128,1600]{2,1,0:T(8,128)(2,1)} all-gather(bf16[1,16,1600]{2,1,0:T(8,128)(2,1)} %copy.234), channel_id=1, replica_groups=mesh['pipe'=4,'dp'=16,'tensor'=8] {'tensor'}, dimensions={1}, use_global_device_ids=true | all-gather | bytes 460800 | tf_op jit(solution)/shard_map/all_gather | solution.py:158
  344.3 32.0 %conditional.7 = (bf16[1,128,1600]{1,2,0:T(8,128)(2,1)}, bf16[1,1,128,768]{3,2,0,1:T(8,128)(2,1)}, bf16[1,1,128,1600]{2,3,0,1:T(8,128)(2,1)}) conditional(s32[]{:T(128)} %convert_element_type.339, () %tuple.72, (s32[]{:T(128)}, bf16[2,1,128,2,128]{4,2,3,0,1:T(8,128)(2,1)}, f32[2,1,2,128,128]{3,4,2,0,1:T(8,128)S(1)}, f32[1,1600]{1,0:T(1,128)S(1)}, ...), branch_computations={%region_11.12_spmd, %region_12.13_spmd} | conditional | flops 454803200 | bytes 11565162 | solution.py:137
  378.3 4.1 all-to-all-start.2
  391.7 4.0 all-to-all-done.2
  411.1 38.8 %collective-permute-done.2 = bf16[1,16,1600]{1,2,0:T(8,128)(2,1)} collective-permute-done((bf16[1,16,1600]{1,2,0:T(8,128)(2,1)S(1)}, bf16[1,16,1600]{1,2,0:T(8,128)(2,1)}, u32[]{:S(2)}, u32[]{:S(2)}) %collective-permute-start.2) | collective-permute-done | bytes 51232 | tf_op jit(solution)/shard_map/ppermute | solution.py:23
  451.8 15.8 %all_gather.22 = bf16[1,128,1600]{2,1,0:T(8,128)(2,1)} all-gather(bf16[1,16,1600]{2,1,0:T(8,128)(2,1)} %copy.249), channel_id=1, replica_groups=mesh['pipe'=4,'dp'=16,'tensor'=8] {'tensor'}, dimensions={1}, use_global_device_ids=true | all-gather | bytes 460800 | tf_op jit(solution)/shard_map/all_gather | solution.py:158
  471.6 32.2 %conditional.8 = (bf16[1,128,1600]{1,2,0:T(8,128)(2,1)}, bf16[1,1,128,768]{3,2,0,1:T(8,128)(2,1)}, bf16[1,1,128,1600]{2,3,0,1:T(8,128)(2,1)}) conditional(s32[]{:T(128)} %convert_element_type.344, () %tuple.74, (s32[]{:T(128)}, bf16[2,1,128,2,128]{4,2,3,0,1:T(8,128)(2,1)}, f32[2,1,2,128,128]{3,4,2,0,1:T(8,128)S(1)}, f32[1,1600]{1,0:T(1,128)S(1)}, ...), branch_computations={%region_15.16_spmd, %region_16.17_spmd} | conditional | flops 454803200 | bytes 11565162 | solution.py:137
  505.9 4.1 all-to-all-start.3
  538.9 2.2 collective-permute-start.3
  544.3 14.5 %collective-permute-done.3 = bf16[1,16,1600]{1,2,0:T(8,128)(2,1)} collective-permute-done((bf16[1,16,1600]{1,2,0:T(8,128)(2,1)}, bf16[1,16,1600]{1,2,0:T(8,128)(2,1)}, u32[]{:S(2)}, u32[]{:S(2)}) %collective-permute-start.3) | collective-permute-done | bytes 51232 | tf_op jit(solution)/shard_map/ppermute | solution.py:23
  560.6 37.5 %all_gather.23 = bf16[1,128,1600]{2,1,0:T(8,128)(2,1)} all-gather(bf16[1,16,1600]{2,1,0:T(8,128)(2,1)} %copy.264), channel_id=1, replica_groups=mesh['pipe'=4,'dp'=16,'tensor'=8] {'tensor'}, dimensions={1}, use_global_device_ids=true | all-gather | bytes 460800 | tf_op jit(solution)/shard_map/all_gather | solution.py:158
  602.1 2.3 conditional.9
  606.5 5.1 all-to-all-start.4
  619.0 85.0 %fusion = bf16[112,1024]{1,0:T(8,128)(2,1)} fusion(bf16[1600,1024]{1,0:T(8,128)(2,1)S(1)} %pad_maximum_fusion.5), kind=kCustom, calls=%all-reduce-scatter | all-reduce-scatter fusion | flops 1835009 | bytes 3508224
  705.0 3.7 collective-permute-start.4
  708.6 4.1 collective-permute-start.5
  722.6 27.0 %psum.14 = f32[2,1600]{1,0:T(2,128)S(1)} all-reduce(f32[2,1600]{1,0:T(2,128)S(1)} %pad_maximum_fusion.6), channel_id=1, replica_groups=mesh['pipe'=4,'dp'=16,'tensor'=8] {'tensor'}, use_global_device_ids=true, to_apply=%region_30.31 | all-reduce | flops 3200 | bytes 25600 | tf_op jit(solution)/shard_map/psum | solution.py:177
  749.6 71.2 %psum.15 = f32[1,2,1600]{2,1,0:T(2,128)} all-reduce(f32[1,2,1600]{2,1,0:T(2,128)S(1)} %bitcast.594), channel_id=1, replica_groups=mesh['pipe'=4,'dp'=16,'tensor'=8] {'dp'}, use_global_device_ids=true, to_apply=%region_31.32 | all-reduce | flops 3200 | bytes 25600 | tf_op jit(solution)/shard_map/psum | solution.py:177
  (240 shorter events, 222.2 us)
Async XLA Ops:
  7.2 71.6 %all-gather.4.cloned.1.call-start = ((), (), s32[]{:S(2)}) async-start(), calls=%async_computation.5 | async-start | bytes 3620864 | tf_op jit(solution)/shard_map/all_gather | solution.py:54
  9.0 18.5 %copy-start.10 = (bf16[2,1,128,1600]{2,3,1,0:T(8,128)(2,1)S(1)}, bf16[2,1,128,1600]{2,3,1,0:T(8,128)(2,1)}, u32[]{:S(2)}) copy-start(bf16[2,1,128,1600]{2,3,1,0:T(8,128)(2,1)} %param.18) | copy-start | bytes 2457604
  27.0 57.4 %copy-start = (bf16[1,2,1,128,1600]{4,3,2,1,0:T(8,128)(2,1)}, bf16[1,2,1,128,1600]{4,3,2,1,0:T(8,128)(2,1)S(1)}, u32[]{:S(2)}) copy-start(bf16[1,2,1,128,1600]{4,3,2,1,0:T(8,128)(2,1)S(1)} %all-gather) | copy-start | bytes 2457604
  27.3 57.2 %copy-start.39 = (f32[2,128]{1,0:T(2,128)}, f32[2,128]{1,0:T(2,128)S(1)}, u32[]{:S(2)}) copy-start(f32[2,128]{1,0:T(2,128)S(1)} %add_rsqrt_fusion) | copy-start | bytes 3076
  28.4 50.4 %copy-start.21 = (bf16[3,1,128,1600]{2,3,0,1:T(8,128)(2,1)}, bf16[3,1,128,1600]{2,3,0,1:T(8,128)(2,1)S(1)}, u32[]{:S(2)}) copy-start(bf16[3,1,128,1600]{2,3,0,1:T(8,128)(2,1)S(1)} %get-tuple-element.409) | copy-start | bytes 3686404
  87.5 4.2 copy-start.26
  91.7 3.9 copy-start.33
  91.8 2.1 copy-start.12
  99.8 18.2 %all-to-all-start = ((bf16[1,8,16,1600]{3,2,0,1:T(8,128)(2,1)}), bf16[1,8,16,1600]{3,2,0,1:T(8,128)(2,1)}, u32[]{:S(2)}, u32[]{:S(2)}) async-start(bf16[1,8,16,1600]{3,2,0,1:T(8,128)(2,1)} %bitcast.589), calls=%async_computation | async-start | bytes 851968 | tf_op jit(solution)/shard_map/all_to_all | solution.py:141
  130.1 42.2 %collective-permute-start = (bf16[1,16,1600]{1,2,0:T(8,128)(2,1)}, bf16[1,16,1600]{1,2,0:T(8,128)(2,1)}, u32[]{:S(2)}, u32[]{:S(2)}) collective-permute-start(bf16[1,16,1600]{1,2,0:T(8,128)(2,1)} %fusion.121), channel_id=1, source_target_pairs={{128,0},{256,128},{384,256},{129,1},{257,129},{385,257},{130,2},{2... | collective-permute-start | bytes 153608 | tf_op jit(solution)/shard_map/ppermute | solution.py:23
  226.4 96.2 %collective-permute-start.1 = (bf16[1,16,1600]{1,2,0:T(8,128)(2,1)}, bf16[1,16,1600]{1,2,0:T(8,128)(2,1)}, u32[]{:S(2)}, u32[]{:S(2)}) collective-permute-start(bf16[1,16,1600]{1,2,0:T(8,128)(2,1)} %fusion.141), channel_id=1, source_target_pairs={{128,0},{256,128},{384,256},{129,1},{257,129},{385,257},{130,2},{2... | collective-permute-start | bytes 153608 | tf_op jit(solution)/shard_map/ppermute | solution.py:23
  378.3 17.4 %all-to-all-start.2 = ((bf16[1,8,16,1600]{3,2,0,1:T(8,128)(2,1)}), bf16[1,8,16,1600]{3,2,0,1:T(8,128)(2,1)}, u32[]{:S(2)}, u32[]{:S(2)}) async-start(bf16[1,8,16,1600]{3,2,0,1:T(8,128)(2,1)} %bitcast.590), calls=%async_computation.2 | async-start | bytes 851968 | tf_op jit(solution)/shard_map/all_to_all | solution.py:141
  405.7 4.8 copy-start.32
  407.9 42.0 %collective-permute-start.2 = (bf16[1,16,1600]{1,2,0:T(8,128)(2,1)S(1)}, bf16[1,16,1600]{1,2,0:T(8,128)(2,1)}, u32[]{:S(2)}, u32[]{:S(2)}) collective-permute-start(bf16[1,16,1600]{1,2,0:T(8,128)(2,1)S(1)} %fusion.136), channel_id=1, source_target_pairs={{128,0},{256,128},{384,256},{129,1},{257,129},{385,257},{130,2},{2... | collective-permute-start | bytes 153608 | tf_op jit(solution)/shard_map/ppermute | solution.py:23
  505.9 20.8 %all-to-all-start.3 = ((bf16[1,8,16,1600]{3,2,0,1:T(8,128)(2,1)}), bf16[1,8,16,1600]{3,2,0,1:T(8,128)(2,1)}, u32[]{:S(2)}, u32[]{:S(2)}) async-start(bf16[1,8,16,1600]{3,2,0,1:T(8,128)(2,1)} %bitcast.591), calls=%async_computation.3 | async-start | bytes 851968 | tf_op jit(solution)/shard_map/all_to_all | solution.py:141
  538.9 19.9 %collective-permute-start.3 = (bf16[1,16,1600]{1,2,0:T(8,128)(2,1)}, bf16[1,16,1600]{1,2,0:T(8,128)(2,1)}, u32[]{:S(2)}, u32[]{:S(2)}) collective-permute-start(bf16[1,16,1600]{1,2,0:T(8,128)(2,1)} %fusion.131), channel_id=1, source_target_pairs={{128,0},{256,128},{384,256},{129,1},{257,129},{385,257},{130,2},{2... | collective-permute-start | bytes 153608 | tf_op jit(solution)/shard_map/ppermute | solution.py:23
  604.4 8.8 %copy-start.1 = (bf16[1,2,1,128,1600]{4,3,2,1,0:T(8,128)(2,1)S(1)}, bf16[1,2,1,128,1600]{4,3,2,1,0:T(8,128)(2,1)}, u32[]{:S(2)}) copy-start(bf16[1,2,1,128,1600]{4,3,2,1,0:T(8,128)(2,1)} %copy-done) | copy-start | bytes 2457604
  604.4 8.8 %copy-start.40 = (f32[2,128]{1,0:T(2,128)S(1)}, f32[2,128]{1,0:T(2,128)}, u32[]{:S(2)}) copy-start(f32[2,128]{1,0:T(2,128)} %copy-done.39) | copy-start | bytes 3076
  606.5 113.7 %all-to-all-start.4 = ((bf16[1,8,16,1600]{3,2,0,1:T(8,128)(2,1)}), bf16[1,8,16,1600]{3,2,0,1:T(8,128)(2,1)}, u32[]{:S(2)}, u32[]{:S(2)}) async-start(bf16[1,8,16,1600]{3,2,0,1:T(8,128)(2,1)} %bitcast.152), calls=%async_computation.4 | async-start | bytes 851968 | tf_op jit(solution)/shard_map/all_to_all | solution.py:141
  613.2 3.7 copy-start.11
  704.0 11.5 %copy-start.20 = (bf16[112,1024]{1,0:T(8,128)(2,1)S(1)}, bf16[112,1024]{1,0:T(8,128)(2,1)}, u32[]{:S(2)}) copy-start(bf16[112,1024]{1,0:T(8,128)(2,1)} %fusion) | copy-start | bytes 688132
  705.0 10.5 %collective-permute-start.4 = (bf16[112,1024]{1,0:T(8,128)(2,1)}, bf16[112,1024]{1,0:T(8,128)(2,1)S(1)}, u32[]{:S(2)}, u32[]{:S(2)}) collective-permute-start(bf16[112,1024]{1,0:T(8,128)(2,1)} %fusion), channel_id=1, source_target_pairs={{0,8},{8,16},{16,24},{24,32},{32,40},{40,48},{48,56},{56,64},{64,7... | collective-permute-start | bytes 688136
  708.6 6.8 collective-permute-start.5
  712.7 3.4 copy-start.19
  712.7 3.4 copy-start.28
  712.7 3.4 copy-start.29
  717.8 4.7 copy-start.35
  717.8 4.7 copy-start.36
  717.8 4.7 copy-start.37
  717.8 4.7 copy-start.38
  722.2 99.2 %copy-start.13 = (bf16[1,128,1600]{1,2,0:T(8,128)(2,1)S(1)}, bf16[1,128,1600]{1,2,0:T(8,128)(2,1)}, u32[]{:S(2)}) copy-start(bf16[1,128,1600]{1,2,0:T(8,128)(2,1)} %get-tuple-element.402) | copy-start | bytes 1228804
  722.2 99.2 %copy-start.41 = (f32[16]{0:T(128)S(1)}, f32[16]{0:T(128)}, u32[]{:S(2)}) copy-start(f32[16]{0:T(128)} %get-tuple-element.429) | copy-start | bytes 196
  (15 other events, 19.7 us)
Sparse Core Ops, SparseCore 0:
  11.6 67.1 all-gather.3

commit v2 on v1

v2 whole, which is shorter than its diff:
```python
import functools
import math

import jax
import jax.numpy as jnp
from jax import lax
from jax.experimental import pallas as pl
from jax.experimental.pallas import tpu as pltpu
from jax.sharding import PartitionSpec as P

HD = 128
D = 1600
ROWS = 100
WIDE = 256
SIDE = 4

beta_one = 0.9
beta_two = 0.95
adam_eps = 1e-08
learn_rate = 0.001
weight_decay = 0.05
adam_step = 100.0
norm_eps = 1e-06

F32 = jnp.float32
BF16 = jnp.bfloat16
MESH = pl.DeviceIdType.MESH


def dot(left, right, dims):
    return lax.dot_general(left, right, ((dims[:1], dims[1:]), ((), ())), preferred_element_type=F32)


def kernel(
    x_ref, og_ref, ls_ref, gain_ref, master_ref, one_ref, two_ref,
    ig_ref, nm_ref, n1_ref, n2_ref, sg_ref,
    wland, dense, wide, xall, normed, qkv, probs, att, outproj, inc, scaled, dproj,
    part, s1land, pair, s2land, own_out, gsend, gland1, gmid, gmid_send, gland2, small, sm_t, sm_d, sm_send,
    w_ss, w_rs, x_ss, x_rs, a_ss, a_rs, c_ss, c_rs, g_ss, g_rs, t_ss, t_rs, d_ss, d_rs,
):
    p = lax.axis_index("pipe")
    r = lax.axis_index("dp")
    t = lax.axis_index("tensor")
    chip = t // 2
    core = t % 2
    y = r // SIDE
    x = r % SIDE
    partner = chip * 2 + (1 - core)
    root = math.sqrt(HD)

    def up(v, by):
        return lax.rem(v + by, SIDE)

    def send(src, dst, ss, rs, where):
        copy = pltpu.make_async_remote_copy(
            src_ref=src, dst_ref=dst, send_sem=ss, recv_sem=rs, device_id=where, device_id_type=MESH
        )
        copy.start()
        return copy

    def landed(dst, rs):
        pltpu.make_async_remote_copy(
            src_ref=dst, dst_ref=dst, send_sem=rs, recv_sem=rs,
            device_id={"tensor": partner}, device_id_type=MESH,
        ).wait_recv()

    for q in range(4):
        wland[q, r] = master_ref[:, q * WIDE : (q + 1) * WIDE].astype(BF16)

    barrier = pltpu.get_barrier_semaphore()
    for k in range(1, 16):
        pl.semaphore_signal(barrier, inc=1, device_id={"dp": lax.rem(r + k, 16)}, device_id_type=MESH)
    for k in range(1, 8):
        pl.semaphore_signal(barrier, inc=1, device_id={"tensor": lax.rem(t + k, 8)}, device_id_type=MESH)
    for k in (1, 3):
        pl.semaphore_signal(barrier, inc=1, device_id={"pipe": lax.rem(p + k, 4)}, device_id_type=MESH)
    pl.semaphore_wait(barrier, 24)

    def at(h, near, far):
        return far * SIDE + near if h == 0 else near * SIDE + far

    def coords(h):
        return (x, y) if h == 0 else (y, x)

    def spread(buf, ss, rs):
        copies = [send(buf.at[t], buf.at[t], ss.at[0], rs.at[t], {"tensor": partner})]
        for k in range(1, 4):
            other = up(chip, k) * 2 + core
            copies.append(send(buf.at[t], buf.at[t], ss.at[k], rs.at[t], {"tensor": other}))
        return copies

    def relay(buf, ss, rs):
        copies = []
        for k in range(1, 4):
            other = up(chip, k) * 2 + core
            landed(buf.at[other], rs.at[other])
            copies.append(send(buf.at[other], buf.at[other], ss.at[3 + k], rs.at[other], {"tensor": partner}))
        return copies

    def settle(buf, rs):
        landed(buf.at[partner], rs.at[partner])
        for k in range(1, 4):
            other = up(chip, k) * 2 + 1 - core
            landed(buf.at[other], rs.at[other])

    pending = []

    def wsend(q, s, slot, where):
        pending.append(send(wland.at[q, s], wland.at[q, s], w_ss.at[q, slot], w_rs.at[q, s], {"dp": where}))

    for h in range(2):
        near, far = coords(h)
        for q in (2 * h, 2 * h + 1):
            wsend(q, r, 0, at(h, up(near, 1), far))
            wsend(q, r, 1, at(h, up(near, 3), far))
    xall[t] = x_ref[...]
    x_copies = spread(xall, x_ss, x_rs)
    for h in range(2):
        near, far = coords(h)
        for q in (2 * h, 2 * h + 1):
            wsend(q, r, 3, at(h, near, up(far, 1)))
            wsend(q, r, 4, at(h, near, up(far, 3)))
    for h in range(2):
        near, far = coords(h)
        for q in (2 * h, 2 * h + 1):
            below = at(h, up(near, 3), far)
            above = at(h, up(near, 1), far)
            landed(wland.at[q, below], w_rs.at[q, below])
            if q % 2 == 0:
                wsend(q, below, 2, above)
            landed(wland.at[q, above], w_rs.at[q, above])
            if q % 2 == 1:
                wsend(q, above, 2, below)
            for j, s in ((1, below), (2, above)):
                wsend(q, s, 3 + 3 * j, at(h, near, up(far, 1)))
                wsend(q, s, 4 + 3 * j, at(h, near, up(far, 3)))
    for h in range(2):
        near, far = coords(h)
        for q in (2 * h, 2 * h + 1):
            s = at(h, up(near, 2), far)
            landed(wland.at[q, s], w_rs.at[q, s])
            wsend(q, s, 12, at(h, near, up(far, 1)))
            wsend(q, s, 13, at(h, near, up(far, 3)))
    x_copies += relay(xall, x_ss, x_rs)
    settle(xall, x_rs)

    gain = gain_ref[...]
    for m in range(2):
        rows = xall[:, m].reshape(128, D).astype(F32)
        inverse = lax.rsqrt(jnp.mean(rows * rows, axis=-1, keepdims=True) + norm_eps)
        normed[m * 128 : (m + 1) * 128] = (rows * inverse * gain).astype(BF16)

    @pl.when(p == 3)
    def _():
        inc[...] = og_ref[...]

    for j, step in enumerate((0, 3, 1, 2)):
        for h in range(2):
            near, far = coords(h)
            for q in (2 * h, 2 * h + 1):
                lower = at(h, up(near, step), up(far, 3))
                upper = at(h, up(near, step), up(far, 1))
                landed(wland.at[q, lower], w_rs.at[q, lower])
                if q % 2 == 0:
                    wsend(q, lower, 5 + 3 * j, at(h, near, up(far, 1)))
                landed(wland.at[q, upper], w_rs.at[q, upper])
                if q % 2 == 1:
                    wsend(q, upper, 5 + 3 * j, at(h, near, up(far, 3)))
    for h in range(2):
        near, far = coords(h)
        for q in (2 * h, 2 * h + 1):
            for step in range(4):
                s = at(h, up(near, step), up(far, 2))
                landed(wland.at[q, s], w_rs.at[q, s])

    for q in range(4):
        for s in range(16):
            wide[s * ROWS : (s + 1) * ROWS] = wland[q, s].astype(F32)
        dense[q] = wide[...].astype(BF16)
        if q < 3:
            qkv[q] = dot(normed[...], dense[q], (1, 0)).astype(BF16)
    for m in range(2):
        row = slice(m * 128, (m + 1) * 128)
        for head in range(2):
            col = slice(head * HD, (head + 1) * HD)
            scores = dot(qkv[0, row, col], qkv[1, row, col], (1, 1)) / root
            scores = jnp.exp(scores - jnp.max(scores, axis=-1, keepdims=True))
            prob = scores / jnp.sum(scores, axis=-1, keepdims=True)
            probs[m, head] = prob
            att[row, col] = dot(prob.astype(BF16), qkv[2, row, col], (1, 0)).astype(BF16)

    def backward(m):
        row = slice(m * 128, (m + 1) * 128)
        scaled_now = (ls_ref[...] * inc[m].reshape(128, D).astype(F32)).astype(BF16)
        scaled[row] = scaled_now
        d_att = dot(scaled_now, dense[3], (1, 0)).astype(BF16)
        for head in range(2):
            col = slice(head * HD, (head + 1) * HD)
            d_now = d_att[:, col]
            d_prob = dot(d_now, qkv[2, row, col], (1, 1))
            delta = jnp.sum(d_now.astype(F32) * att[row, col].astype(F32), axis=-1, keepdims=True)
            prob = probs[m, head]
            d_score = (prob * (d_prob - delta) / root).astype(BF16)
            dproj[0, row, col] = dot(d_score, qkv[1, row, col], (1, 0)).astype(BF16)
            dproj[1, row, col] = dot(d_score, qkv[0, row, col], (0, 0)).astype(BF16)
            dproj[2, row, col] = dot(prob.astype(BF16), d_now, (0, 0)).astype(BF16)
        total = dot(dproj[0, row], dense[0], (1, 1))
        total += dot(dproj[1, row], dense[1], (1, 1))
        total += dot(dproj[2, row], dense[2], (1, 1))
        total = total.astype(BF16)
        for other in range(8):
            part[m, other % 2, other // 2] = total[other * 16 : (other + 1) * 16]

    def scale_part(m):
        row = slice(m * 128, (m + 1) * 128)
        out_rows = dot(att[row], dense[3], (1, 1))
        return jnp.sum(inc[m].reshape(128, D).astype(F32) * out_rows, axis=0, keepdims=True)

    def first_stage(m):
        return [
            send(part.at[m, 1 - core], s1land.at[m], c_ss.at[m, 0], c_rs.at[m, 0], {"tensor": partner})
        ]

    def second_stage(m):
        landed(s1land.at[m], c_rs.at[m, 0])
        pair[m] = (part[m, core].astype(F32) + s1land[m].astype(F32)).astype(BF16)
        copies = []
        for k in range(1, 4):
            to = up(chip, k)
            copies.append(
                send(pair.at[m, to], s2land.at[m, chip], c_ss.at[m, k], c_rs.at[m, 1 + chip], {"tensor": to * 2 + core})
            )
        return copies

    def finish(m):
        total = pair[m, chip].astype(F32)
        for k in range(1, 4):
            other = up(chip, k)
            landed(s2land.at[m, other], c_rs.at[m, 1 + other])
            total += s2land[m, other].astype(F32)
        rows = x_ref[m].astype(F32)
        inverse = lax.rsqrt(jnp.mean(rows * rows, axis=-1, keepdims=True) + norm_eps)
        unit = rows * inverse
        e = total * gain
        d_input = inverse * (e - unit * jnp.mean(e * unit, axis=-1, keepdims=True))
        passed = (inc[m, t].astype(F32) + d_input).astype(BF16)
        own_out[m] = passed
        ig_ref[m] = passed
        return jnp.sum(total * unit, axis=0, keepdims=True)

    def hand_on(m):
        return pltpu.make_async_remote_copy(
            src_ref=own_out.at[m], dst_ref=inc.at[m, t], send_sem=c_ss.at[m, 4], recv_sem=a_rs.at[m, t],
            device_id={"pipe": lax.rem(p + 3, 4)}, device_id_type=MESH,
        )

    def take_in(m):
        @pl.when(p < 3)
        def _():
            landed(inc.at[m, t], a_rs.at[m, t])
            copies = spread(inc.at[m], a_ss.at[m], a_rs.at[m])
            copies += relay(inc.at[m], a_ss.at[m], a_rs.at[m])
            settle(inc.at[m], a_rs.at[m])
            for copy in copies:
                copy.wait_send()

    scale_sum = jnp.zeros((1, D), F32)
    gain_sum = jnp.zeros((1, D), F32)
    for m in range(2):
        take_in(m)
        backward(m)
        pending += first_stage(m)
        pending += second_stage(m)
        scale_sum += scale_part(m)
        gain_sum += finish(m)

        @pl.when(p > 0)
        def _():
            hand_on(m).start()

    small[0:1] = scale_sum
    small[1:2] = gain_sum
    for k in range(1, 8):
        other = lax.rem(t + k, 8)
        pending.append(send(small, sm_t.at[t], t_ss.at[k], t_rs.at[t], {"tensor": other}))

    for copy in pending[:60]:
        copy.wait_send()
    pending = pending[60:]
    for q in (3, 0, 1, 2):
        h = q // 2
        if q == 3:
            wide[...] = dot(scaled[...], att[...], (0, 0))
        else:
            wide[...] = dot(normed[...], dproj[q], (0, 0))
        for s in range(16):
            place = s if h == 0 else (s % SIDE) * SIDE + s // SIDE
            gsend[q, place // SIDE, place % SIDE] = wide[s * ROWS : (s + 1) * ROWS].astype(BF16)

    def gcopy(q, kind, src, where, second):
        h = q // 2
        near, far = coords(h)
        if second:
            to = at(h, up(near, where), far)
            slot, land = 3 + kind, gland2.at[q, kind]
        else:
            to = at(h, near, up(far, where))
            slot, land = kind, gland1.at[q, kind]
        pending.append(send(src, land, g_ss.at[q, slot], g_rs.at[q, slot], {"dp": to}))

    order = (3, 0, 1, 2)
    for q in order:
        near, far = coords(q // 2)
        ahead, back = (1, 3) if q % 2 == 0 else (3, 1)
        gcopy(q, 0, gsend.at[q, up(far, 2)], ahead, False)
        gcopy(q, 1, gsend.at[q, up(far, back)], back, False)
    for q in order:
        near, far = coords(q // 2)
        ahead, back = (1, 3) if q % 2 == 0 else (3, 1)
        landed(gland1.at[q, 0], g_rs.at[q, 0])
        line = up(far, ahead)
        gsend[q, line] = (gsend[q, line].astype(F32) + gland1[q, 0].astype(F32)).astype(BF16)
        gcopy(q, 2, gsend.at[q, line], ahead, False)

    total = small[...]
    for k in range(1, 8):
        other = lax.rem(t + k, 8)
        landed(sm_t.at[other], t_rs.at[other])
        total += sm_t[other]
    sm_send[...] = total
    for k in range(1, 16):
        other = lax.rem(r + k, 16)
        pending.append(send(sm_send, sm_d.at[r], d_ss.at[k], d_rs.at[r], {"dp": other}))

    for q in order:
        near, far = coords(q // 2)
        ahead, back = (1, 3) if q % 2 == 0 else (3, 1)
        landed(gland1.at[q, 1], g_rs.at[q, 1])
        landed(gland1.at[q, 2], g_rs.at[q, 2])
        gmid[q] = gsend[q, far].astype(F32) + gland1[q, 1].astype(F32) + gland1[q, 2].astype(F32)
        gmid_send[q] = gmid[q].astype(BF16)
        gcopy(q, 0, gmid_send.at[q, up(near, 2)], ahead, True)
        gcopy(q, 1, gmid_send.at[q, up(near, back)], back, True)
    for q in order:
        near, far = coords(q // 2)
        ahead, back = (1, 3) if q % 2 == 0 else (3, 1)
        landed(gland2.at[q, 0], g_rs.at[q, 3])
        line = up(near, ahead)
        gmid_send[q, line] = (gmid[q, line] + gland2[q, 0].astype(F32)).astype(BF16)
        gcopy(q, 2, gmid_send.at[q, line], ahead, True)

    bias_one = 1.0 - beta_one**adam_step
    bias_two = 1.0 - beta_two**adam_step
    for q in order:
        near, far = coords(q // 2)
        landed(gland2.at[q, 1], g_rs.at[q, 4])
        landed(gland2.at[q, 2], g_rs.at[q, 5])
        grad = gmid[q, near] + gland2[q, 1].astype(F32) + gland2[q, 2].astype(F32)
        cols = slice(q * WIDE, (q + 1) * WIDE)
        first = beta_one * one_ref[:, cols] + (1.0 - beta_one) * grad
        second = beta_two * two_ref[:, cols] + (1.0 - beta_two) * grad * grad
        update = first / bias_one / (jnp.sqrt(second / bias_two) + adam_eps)
        old = master_ref[:, cols]
        nm_ref[:, cols] = old - learn_rate * (update + weight_decay * old)
        n1_ref[:, cols] = first
        n2_ref[:, cols] = second

    total = sm_send[...]
    for k in range(1, 16):
        other = lax.rem(r + k, 16)
        landed(sm_d.at[other], d_rs.at[other])
        total += sm_d[other]
    sg_ref[...] = total

    for copy in pending + x_copies:
        copy.wait_send()

    @pl.when(p > 0)
    def _():
        for m in range(2):
            hand_on(m).wait_send()


def local(x_in, out_grad, layer_scale, norm_gain, master, moment_one, moment_two):
    vmem = pl.BlockSpec(memory_space=pltpu.VMEM)
    shard = jax.ShapeDtypeStruct((ROWS, 4 * WIDE), F32)
    dma = pltpu.SemaphoreType.DMA
    scratch = [
        pltpu.VMEM((4, 16, ROWS, WIDE), BF16),
        pltpu.VMEM((4, D, WIDE), BF16),
        pltpu.VMEM((D, WIDE), F32),
        pltpu.VMEM((8, 2, 16, D), BF16),
        pltpu.VMEM((256, D), BF16),
        pltpu.VMEM((3, 256, WIDE), BF16),
        pltpu.VMEM((2, 2, 128, 128), F32),
        pltpu.VMEM((256, WIDE), BF16),
        pltpu.VMEM((8, 128), F32),
        pltpu.VMEM((2, 8, 16, D), BF16),
        pltpu.VMEM((256, D), BF16),
        pltpu.VMEM((3, 256, WIDE), BF16),
        pltpu.VMEM((2, 2, 4, 16, D), BF16),
        pltpu.VMEM((2, 4, 16, D), BF16),
        pltpu.VMEM((2, 4, 16, D), BF16),
        pltpu.VMEM((2, 4, 16, D), BF16),
        pltpu.VMEM((2, 16, D), BF16),
        pltpu.VMEM((4, 4, 4, ROWS, WIDE), BF16),
        pltpu.VMEM((4, 3, 4, ROWS, WIDE), BF16),
        pltpu.VMEM((4, 4, ROWS, WIDE), F32),
        pltpu.VMEM((4, 4, ROWS, WIDE), BF16),
        pltpu.VMEM((4, 3, ROWS, WIDE), BF16),
        pltpu.VMEM((2, D), F32),
        pltpu.VMEM((8, 2, D), F32),
        pltpu.VMEM((16, 2, D), F32),
        pltpu.VMEM((2, D), F32),
        dma((4, 15)), dma((4, 16)),
        dma((7,)), dma((8,)),
        dma((2, 7)), dma((2, 8)),
        dma((2, 5)), dma((2, 5)),
        dma((4, 6)), dma((4, 6)),
        dma((8,)), dma((8,)),
        dma((16,)), dma((16,)),
    ]
    outs = pl.pallas_call(
        kernel,
        out_shape=(
            jax.ShapeDtypeStruct((2, 16, D), BF16),
            shard,
            shard,
            shard,
            jax.ShapeDtypeStruct((2, D), F32),
        ),
        in_specs=[vmem] * 7,
        out_specs=(vmem,) * 5,
        scratch_shapes=scratch,
        compiler_params=pltpu.CompilerParams(
            collective_id=0, has_side_effects=True, vmem_limit_bytes=56 * 1024 * 1024
        ),
        cost_estimate=pl.CostEstimate(flops=3 * 10**9, bytes_accessed=10**7, transcendentals=10**5),
    )(
        x_in.reshape(2, 16, D),
        out_grad.reshape(2, 8, 16, D),
        layer_scale,
        norm_gain,
        master[0],
        moment_one[0],
        moment_two[0],
    )
    grads, new_master, first, second, scales = outs
    return (grads.reshape(1, 2, 1, 16, D), new_master[None], first[None], second[None], scales[None])


def solution(mesh):
    placed = (
        P("pipe", None, "dp", "tensor", None),
        P(None, "dp", None, None),
        P("pipe", None),
        P("pipe", None),
        P("pipe", "dp", "tensor"),
        P("pipe", "dp", "tensor"),
        P("pipe", "dp", "tensor"),
    )
    return jax.shard_map(
        local,
        mesh=mesh,
        in_specs=placed,
        out_specs=(
            P("pipe", None, "dp", "tensor", None),
            P("pipe", "dp", "tensor"),
            P("pipe", "dp", "tensor"),
            P("pipe", "dp", "tensor"),
            P("pipe", None, None),
        ),
        check_vma=False,
    )
```

time: 842 us -> 182 us (0.22)
  the two profiles are of different devices: /device:TPU:128 before, /device:TPU:64 now
where the time goes in v2:
time: 182 us
  Pallas kernels  171 us (94%)
  local copies, waits for them, and re-layouts  10.1 us (6%)
    pallas_call x1, Pallas kernels, local(): pl.pallas_call(kernel, out_shape=(jax.ShapeDtypeStruct((2, 16, D), BF16),...  171 us
    unnamed x22, local copies, waits for them, and re-layouts  10.1 us

profile of v2, /device:TPU:64, one launch (start us, length us, event | category | flops | bytes accessed | tf_op | source)
XLA Modules:
  0.0 181.5 jit_solution(4945797223143292474)
XLA Ops:
  0.6 0.0 copy-start
  0.6 1.9 %copy.23 = f32[1,100,1024]{2,1,0:T(8,128)} copy(f32[1,100,1024]{2,0,1:T(1,128)} %param.11) | data formatting | bytes 819200
  2.6 0.0 copy-done
  2.6 0.0 copy-start.3
  2.6 0.0 copy-start.4
  2.6 1.3 copy.12
  3.8 0.0 copy-done.3
  3.8 0.0 copy-done.4
  3.8 1.1 copy_bitcast_fusion
  4.9 170.7 %shard_map.110 = (bf16[2,16,1600]{2,1,0:T(8,128)(2,1)}, f32[100,1024]{1,0:T(8,128)}, f32[100,1024]{1,0:T(8,128)}, f32[100,1024]{1,0:T(8,128)}, f32[2,1600]{1,0:T(2,128)}) custom-call(bf16[2,16,1600]{2,1,0:T(8,128)(2,1)} %bitcast.23, bf16[2,8,16,1600]{3,2,1,0:T(8,128)(2,1)} %bitcast.16, f32[1,1600]{1,0:T(1,128)} %ls_ref.1, f32[1,1600]{1,0:T(1,128)} %gain_ref.1, ...), custom_call_target="tpu_custom_call" | custom-call | flops 3000000000 | bytes 10000000 | tf_op jit(solution)/shard_map/pallas_call | solution.py:423
  175.6 0.0 copy-start.2
  175.6 2.2 %copy.14 = f32[1,100,1024]{2,0,1:T(1,128)} copy(f32[1,100,1024]{2,1,0:T(8,128)} %bitcast.20) | data formatting | bytes 819200
  177.9 0.0 copy-done.2
  177.9 0.0 copy-start.1
  177.9 1.2 copy.15
  179.0 0.0 copy-done.1
  179.0 0.0 copy-start.5
  179.0 1.2 copy.16
  180.2 0.0 copy-done.5
  180.2 0.0 copy-start.6
  180.2 0.6 copy.26
  180.9 0.1 copy-done.6
  180.9 0.6 copy.27
Async XLA Ops:
  0.6 1.9 %copy-start = (bf16[2,1,128,1600]{2,3,1,0:T(8,128)(2,1)S(1)}, bf16[2,1,128,1600]{2,3,1,0:T(8,128)(2,1)}, u32[]{:S(2)}) copy-start(bf16[2,1,128,1600]{2,3,1,0:T(8,128)(2,1)} %param.8) | copy-start | bytes 2457604
  2.6 1.3 copy-start.3
  2.6 1.3 copy-start.4
  175.6 2.2 %copy-start.2 = (f32[100,1024]{1,0:T(8,128)S(1)}, f32[100,1024]{1,0:T(8,128)}, u32[]{:S(2)}) copy-start(f32[100,1024]{1,0:T(8,128)} %get-tuple-element.12) | copy-start | bytes 1228804
  177.9 1.2 copy-start.1
  179.0 1.2 copy-start.5
  180.2 0.7 copy-start.6

commit v3 on v2

--- a/solution.py
+++ b/solution.py
@@ -32,11 +32,11 @@
 
 
 def kernel(
-    x_ref, og_ref, ls_ref, gain_ref, master_ref, one_ref, two_ref,
-    ig_ref, nm_ref, n1_ref, n2_ref, sg_ref,
-    wland, dense, wide, xall, normed, qkv, probs, att, outproj, inc, scaled, dproj,
-    part, s1land, pair, s2land, own_out, gsend, gland1, gmid, gmid_send, gland2, small, sm_t, sm_d, sm_send,
-    w_ss, w_rs, x_ss, x_rs, a_ss, a_rs, c_ss, c_rs, g_ss, g_rs, t_ss, t_rs, d_ss, d_rs,
+    x_ref, og_ref, ls_ref, gain_ref, master_ref,
+    ig_ref, grad_ref, sg_ref,
+    wload, wland, dense, wide, xall, normed, flat, qkv, probs, att, inc, scaled, dproj,
+    part, s1land, arrived, passing, running, own_out, gsend, gland1, gmid, gmid_send, gland2, small, sm_t, sm_d, sm_send,
+    m_s, w_ss, w_rs, x_ss, x_rs, a_ss, a_rs, c_ss, c_rs, r_ss, r_rs, o_ss, o_rs, g_ss, g_rs, t_ss, t_rs, d_ss, d_rs,
 ):
     p = lax.axis_index("pipe")
     r = lax.axis_index("dp")
@@ -46,6 +46,7 @@
     y = r // SIDE
     x = r % SIDE
     partner = chip * 2 + (1 - core)
+    mirror = (3 - chip) * 2 + core
     root = math.sqrt(HD)
 
     def up(v, by):
@@ -64,8 +65,10 @@
             device_id={"tensor": partner}, device_id_type=MESH,
         ).wait_recv()
 
-    for q in range(4):
-        wland[q, r] = master_ref[:, q * WIDE : (q + 1) * WIDE].astype(BF16)
+    loads = []
+    for b in range(8):
+        loads.append(pltpu.make_async_copy(master_ref.at[:, b], wload.at[b], m_s.at[b]))
+        loads[b].start()
 
     barrier = pltpu.get_barrier_semaphore()
     for k in range(1, 16):
@@ -73,7 +76,13 @@
     for k in range(1, 8):
         pl.semaphore_signal(barrier, inc=1, device_id={"tensor": lax.rem(t + k, 8)}, device_id_type=MESH)
     for k in (1, 3):
-        pl.semaphore_signal(barrier, inc=1, device_id={"pipe": lax.rem(p + k, 4)}, device_id_type=MESH)
+        pl.semaphore_signal(
+            barrier, inc=1, device_id={"pipe": lax.rem(p + k, 4), "tensor": mirror}, device_id_type=MESH
+        )
+    for q in range(4):
+        loads[2 * q].wait()
+        loads[2 * q + 1].wait()
+        wland[q, r] = jnp.concatenate([wload[2 * q], wload[2 * q + 1]], axis=1).astype(BF16)
     pl.semaphore_wait(barrier, 24)
 
     def at(h, near, far):
@@ -141,19 +150,6 @@
             landed(wland.at[q, s], w_rs.at[q, s])
             wsend(q, s, 12, at(h, near, up(far, 1)))
             wsend(q, s, 13, at(h, near, up(far, 3)))
-    x_copies += relay(xall, x_ss, x_rs)
-    settle(xall, x_rs)
-
-    gain = gain_ref[...]
-    for m in range(2):
-        rows = xall[:, m].reshape(128, D).astype(F32)
-        inverse = lax.rsqrt(jnp.mean(rows * rows, axis=-1, keepdims=True) + norm_eps)
-        normed[m * 128 : (m + 1) * 128] = (rows * inverse * gain).astype(BF16)
-
-    @pl.when(p == 3)
-    def _():
-        inc[...] = og_ref[...]
-
     for j, step in enumerate((0, 3, 1, 2)):
         for h in range(2):
             near, far = coords(h)
@@ -166,6 +162,22 @@
                 landed(wland.at[q, upper], w_rs.at[q, upper])
                 if q % 2 == 1:
                     wsend(q, upper, 5 + 3 * j, at(h, near, up(far, 3)))
+    x_copies += relay(xall, x_ss, x_rs)
+    settle(xall, x_rs)
+
+    gain = gain_ref[...]
+    for m in range(2):
+        rows = xall[:, m].reshape(128, D).astype(F32)
+        inverse = lax.rsqrt(jnp.mean(rows * rows, axis=-1, keepdims=True) + norm_eps)
+        normed[m * 128 : (m + 1) * 128] = (rows * inverse * gain).astype(BF16)
+
+    @pl.when(p == 3)
+    def _():
+        for m in range(2):
+            inc[m] = og_ref[m].T.reshape(8, 16, D)
+
+    flat[...] = normed[...].T
+
     for h in range(2):
         near, far = coords(h)
         for q in (2 * h, 2 * h + 1):
@@ -216,111 +228,162 @@
         out_rows = dot(att[row], dense[3], (1, 1))
         return jnp.sum(inc[m].reshape(128, D).astype(F32) * out_rows, axis=0, keepdims=True)
 
+    def remote(src, dst, ss, rs, to):
+        return pltpu.make_async_remote_copy(
+            src_ref=src, dst_ref=dst, send_sem=ss, recv_sem=rs, device_id=to, device_id_type=MESH
+        )
+
+    below = {"tensor": lax.rem(t + 6, 8)}
+    section_below = {"pipe": lax.rem(p + 3, 4), "tensor": mirror}
+
     def first_stage(m):
-        return [
-            send(part.at[m, 1 - core], s1land.at[m], c_ss.at[m, 0], c_rs.at[m, 0], {"tensor": partner})
-        ]
-
-    def second_stage(m):
-        landed(s1land.at[m], c_rs.at[m, 0])
-        pair[m] = (part[m, core].astype(F32) + s1land[m].astype(F32)).astype(BF16)
-        copies = []
-        for k in range(1, 4):
-            to = up(chip, k)
-            copies.append(
-                send(pair.at[m, to], s2land.at[m, chip], c_ss.at[m, k], c_rs.at[m, 1 + chip], {"tensor": to * 2 + core})
-            )
-        return copies
-
-    def finish(m):
-        total = pair[m, chip].astype(F32)
-        for k in range(1, 4):
-            other = up(chip, k)
-            landed(s2land.at[m, other], c_rs.at[m, 1 + other])
-            total += s2land[m, other].astype(F32)
-        rows = x_ref[m].astype(F32)
-        inverse = lax.rsqrt(jnp.mean(rows * rows, axis=-1, keepdims=True) + norm_eps)
-        unit = rows * inverse
-        e = total * gain
-        d_input = inverse * (e - unit * jnp.mean(e * unit, axis=-1, keepdims=True))
-        passed = (inc[m, t].astype(F32) + d_input).astype(BF16)
-        own_out[m] = passed
-        ig_ref[m] = passed
-        return jnp.sum(total * unit, axis=0, keepdims=True)
-
-    def hand_on(m):
+        return remote(part.at[m, 1 - core], s1land.at[m], c_ss.at[m], c_rs.at[m], {"tensor": partner})
+
+    def across(m, j):
+        i = 2 * j + core
+        return remote(inc.at[m, i], inc.at[m, i], a_ss.at[m, j], a_rs.at[m, i], {"tensor": partner})
+
+    def down(m, j):
+        i = 2 * j + core
+        return remote(inc.at[m, i], inc.at[m, i], a_ss.at[m, 4 + j], a_rs.at[m, i], below)
+
+    def sum_down(m, j):
+        return remote(passing.at[m, j], arrived.at[m, j], r_ss.at[m, j], r_rs.at[m, j], below)
+
+    def hand_on(m, j):
+        return remote(passing.at[m, j], inc.at[m, 2 * j + core], r_ss.at[m, j], a_rs.at[m, 2 * j + core], section_below)
+
+    def give_back(m, j):
+        return remote(passing.at[m, j], own_out.at[m], o_ss.at[m, j], o_rs.at[m], {"tensor": 2 * j + core})
+
+    def take_piece(m, j):
+        landed(inc.at[m, 2 * j + core], a_rs.at[m, 2 * j + core])
+
+        @pl.when(chip > 0)
+        def _():
+            down(m, j).start()
+
+        across(m, j).start()
+
+    def take_rest(m):
+        for j in range(4):
+            landed(inc.at[m, 2 * j + 1 - core], a_rs.at[m, 2 * j + 1 - core])
+
+    def reduce_start(m):
+        landed(s1land.at[m], c_rs.at[m])
+
+    def reduce_piece(m, j):
+        running[...] = part[m, core, j].astype(F32) + s1land[m, j].astype(F32)
+
+        @pl.when(chip < 3)
+        def _():
+            landed(arrived.at[m, j], r_rs.at[m, j])
+            running[...] += arrived[m, j].astype(F32)
+
+        @pl.when(chip > 0)
+        def _():
+            passing[m, j] = running[...].astype(BF16)
+            sum_down(m, j).start()
+
+        @pl.when(chip == 0)
+        def _():
+            i = 2 * j + core
+            total = running[...]
+            rows = xall[i, m].astype(F32)
+            inverse = lax.rsqrt(jnp.mean(rows * rows, axis=-1, keepdims=True) + norm_eps)
+            unit = rows * inverse
+            e = total * gain
+            d_input = inverse * (e - unit * jnp.mean(e * unit, axis=-1, keepdims=True))
+            passing[m, j] = (inc[m, i].astype(F32) + d_input).astype(BF16)
+
+            @pl.when(p > 0)
+            def _():
+                hand_on(m, j).start()
+
+            if j > 0:
+                give_back(m, j).start()
+            small[1:2] += jnp.sum(total * unit, axis=0, keepdims=True)
+
+    def gcopy(q, kind, second):
+        near, far = coords(q // 2)
+        ahead, back = (1, 3) if q % 2 == 0 else (3, 1)
+        where = back if kind == 1 else ahead
+        owner = (2, back, ahead)[kind]
+        if second:
+            to = at(q // 2, up(near, where), far)
+            src, slot, land = gmid_send.at[q, up(near, owner)], 3 + kind, gland2.at[q, kind]
+        else:
+            to = at(q // 2, near, up(far, where))
+            src, slot, land = gsend.at[q, up(far, owner)], kind, gland1.at[q, kind]
         return pltpu.make_async_remote_copy(
-            src_ref=own_out.at[m], dst_ref=inc.at[m, t], send_sem=c_ss.at[m, 4], recv_sem=a_rs.at[m, t],
-            device_id={"pipe": lax.rem(p + 3, 4)}, device_id_type=MESH,
+            src_ref=src, dst_ref=land, send_sem=g_ss.at[q, slot], recv_sem=g_rs.at[q, slot],
+            device_id={"dp": to}, device_id_type=MESH,
         )
 
-    def take_in(m):
-        @pl.when(p < 3)
-        def _():
-            landed(inc.at[m, t], a_rs.at[m, t])
-            copies = spread(inc.at[m], a_ss.at[m], a_rs.at[m])
-            copies += relay(inc.at[m], a_ss.at[m], a_rs.at[m])
-            settle(inc.at[m], a_rs.at[m])
-            for copy in copies:
-                copy.wait_send()
-
-    scale_sum = jnp.zeros((1, D), F32)
-    gain_sum = jnp.zeros((1, D), F32)
-    for m in range(2):
-        take_in(m)
-        backward(m)
-        pending += first_stage(m)
-        pending += second_stage(m)
-        scale_sum += scale_part(m)
-        gain_sum += finish(m)
-
-        @pl.when(p > 0)
-        def _():
-            hand_on(m).start()
-
-    small[0:1] = scale_sum
-    small[1:2] = gain_sum
+    order = (3, 0, 1, 2)
+
+    def weight_grads():
+        for q in order:
+            if q == 3:
+                wide[...] = dot(scaled[...], att[...], (0, 0))
+            else:
+                wide[...] = dot(flat[...], dproj[q], (1, 0))
+            for s in range(16):
+                place = s if q < 2 else (s % SIDE) * SIDE + s // SIDE
+                gsend[q, place // SIDE, place % SIDE] = wide[s * ROWS : (s + 1) * ROWS].astype(BF16)
+            gcopy(q, 0, False).start()
+            gcopy(q, 1, False).start()
+
+    small[...] = jnp.zeros((2, D), F32)
+
+    @pl.when(p == 3)
+    def _():
+        for m in range(2):
+            backward(m)
+            first_stage(m).start()
+        reduce_start(0)
+        for j in range(4):
+            reduce_piece(0, j)
+
+    @pl.when(p < 3)
+    def _():
+        for j in range(4):
+            take_piece(0, j)
+        take_rest(0)
+        backward(0)
+        first_stage(0).start()
+        reduce_start(0)
+        for j in range(4):
+            reduce_piece(0, j)
+        for j in range(4):
+            take_piece(1, j)
+        take_rest(1)
+        backward(1)
+        first_stage(1).start()
+
+        @pl.when(p == 0)
+        def _():
+            weight_grads()
+
+    reduce_start(1)
+    for j in range(4):
+        reduce_piece(1, j)
+
+    small[0:1] = scale_part(0) + scale_part(1)
     for k in range(1, 8):
         other = lax.rem(t + k, 8)
         pending.append(send(small, sm_t.at[t], t_ss.at[k], t_rs.at[t], {"tensor": other}))
 
-    for copy in pending[:60]:
-        copy.wait_send()
-    pending = pending[60:]
-    for q in (3, 0, 1, 2):
-        h = q // 2
-        if q == 3:
-            wide[...] = dot(scaled[...], att[...], (0, 0))
-        else:
-            wide[...] = dot(normed[...], dproj[q], (0, 0))
-        for s in range(16):
-            place = s if h == 0 else (s % SIDE) * SIDE + s // SIDE
-            gsend[q, place // SIDE, place % SIDE] = wide[s * ROWS : (s + 1) * ROWS].astype(BF16)
-
-    def gcopy(q, kind, src, where, second):
-        h = q // 2
-        near, far = coords(h)
-        if second:
-            to = at(h, up(near, where), far)
-            slot, land = 3 + kind, gland2.at[q, kind]
-        else:
-            to = at(h, near, up(far, where))
-            slot, land = kind, gland1.at[q, kind]
-        pending.append(send(src, land, g_ss.at[q, slot], g_rs.at[q, slot], {"dp": to}))
-
-    order = (3, 0, 1, 2)
+    @pl.when(p > 0)
+    def _():
+        weight_grads()
+
     for q in order:
         near, far = coords(q // 2)
-        ahead, back = (1, 3) if q % 2 == 0 else (3, 1)
-        gcopy(q, 0, gsend.at[q, up(far, 2)], ahead, False)
-        gcopy(q, 1, gsend.at[q, up(far, back)], back, False)
-    for q in order:
-        near, far = coords(q // 2)
-        ahead, back = (1, 3) if q % 2 == 0 else (3, 1)
+        line = up(far, 1 if q % 2 == 0 else 3)
         landed(gland1.at[q, 0], g_rs.at[q, 0])
-        line = up(far, ahead)
         gsend[q, line] = (gsend[q, line].astype(F32) + gland1[q, 0].astype(F32)).astype(BF16)
-        gcopy(q, 2, gsend.at[q, line], ahead, False)
+        gcopy(q, 2, False).start()
 
     total = small[...]
     for k in range(1, 8):
@@ -334,36 +397,25 @@
 
     for q in order:
         near, far = coords(q // 2)
-        ahead, back = (1, 3) if q % 2 == 0 else (3, 1)
         landed(gland1.at[q, 1], g_rs.at[q, 1])
         landed(gland1.at[q, 2], g_rs.at[q, 2])
         gmid[q] = gsend[q, far].astype(F32) + gland1[q, 1].astype(F32) + gland1[q, 2].astype(F32)
         gmid_send[q] = gmid[q].astype(BF16)
-        gcopy(q, 0, gmid_send.at[q, up(near, 2)], ahead, True)
-        gcopy(q, 1, gmid_send.at[q, up(near, back)], back, True)
+        gcopy(q, 0, True).start()
+        gcopy(q, 1, True).start()
     for q in order:
         near, far = coords(q // 2)
-        ahead, back = (1, 3) if q % 2 == 0 else (3, 1)
+        line = up(near, 1 if q % 2 == 0 else 3)
         landed(gland2.at[q, 0], g_rs.at[q, 3])
-        line = up(near, ahead)
         gmid_send[q, line] = (gmid[q, line] + gland2[q, 0].astype(F32)).astype(BF16)
-        gcopy(q, 2, gmid_send.at[q, line], ahead, True)
-
-    bias_one = 1.0 - beta_one**adam_step
-    bias_two = 1.0 - beta_two**adam_step
+        gcopy(q, 2, True).start()
     for q in order:
         near, far = coords(q // 2)
         landed(gland2.at[q, 1], g_rs.at[q, 4])
         landed(gland2.at[q, 2], g_rs.at[q, 5])
-        grad = gmid[q, near] + gland2[q, 1].astype(F32) + gland2[q, 2].astype(F32)
-        cols = slice(q * WIDE, (q + 1) * WIDE)
-        first = beta_one * one_ref[:, cols] + (1.0 - beta_one) * grad
-        second = beta_two * two_ref[:, cols] + (1.0 - beta_two) * grad * grad
-        update = first / bias_one / (jnp.sqrt(second / bias_two) + adam_eps)
-        old = master_ref[:, cols]
-        nm_ref[:, cols] = old - learn_rate * (update + weight_decay * old)
-        n1_ref[:, cols] = first
-        n2_ref[:, cols] = second
+        grad_ref[:, q * WIDE : (q + 1) * WIDE] = (
+            gmid[q, near] + gland2[q, 1].astype(F32) + gland2[q, 2].astype(F32)
+        )
 
     total = sm_send[...]
     for k in range(1, 16):
@@ -374,27 +426,56 @@
 
     for copy in pending + x_copies:
         copy.wait_send()
-
-    @pl.when(p > 0)
-    def _():
-        for m in range(2):
-            hand_on(m).wait_send()
+    for q in order:
+        for kind in range(3):
+            gcopy(q, kind, False).wait_send()
+            gcopy(q, kind, True).wait_send()
+
+    for m in range(2):
+        first_stage(m).wait_send()
+
+        @pl.when(p < 3)
+        def _():
+            for j in range(4):
+                across(m, j).wait_send()
+
+                @pl.when(chip > 0)
+                def _():
+                    down(m, j).wait_send()
+
+        @pl.when(chip > 0)
+        def _():
+            for j in range(4):
+                sum_down(m, j).wait_send()
+            landed(own_out.at[m], o_rs.at[m])
+            ig_ref[m] = own_out[m]
+
+        @pl.when(chip == 0)
+        def _():
+            ig_ref[m] = passing[m, 0]
+            for j in range(1, 4):
+                give_back(m, j).wait_send()
+
+            @pl.when(p > 0)
+            def _():
+                for j in range(4):
+                    hand_on(m, j).wait_send()
 
 
 def local(x_in, out_grad, layer_scale, norm_gain, master, moment_one, moment_two):
     vmem = pl.BlockSpec(memory_space=pltpu.VMEM)
-    shard = jax.ShapeDtypeStruct((ROWS, 4 * WIDE), F32)
     dma = pltpu.SemaphoreType.DMA
     scratch = [
+        pltpu.VMEM((8, ROWS, 128), F32),
         pltpu.VMEM((4, 16, ROWS, WIDE), BF16),
         pltpu.VMEM((4, D, WIDE), BF16),
         pltpu.VMEM((D, WIDE), F32),
         pltpu.VMEM((8, 2, 16, D), BF16),
         pltpu.VMEM((256, D), BF16),
+        pltpu.VMEM((D, 256), BF16),
         pltpu.VMEM((3, 256, WIDE), BF16),
         pltpu.VMEM((2, 2, 128, 128), F32),
         pltpu.VMEM((256, WIDE), BF16),
-        pltpu.VMEM((8, 128), F32),
         pltpu.VMEM((2, 8, 16, D), BF16),
         pltpu.VMEM((256, D), BF16),
         pltpu.VMEM((3, 256, WIDE), BF16),
@@ -402,6 +483,7 @@
         pltpu.VMEM((2, 4, 16, D), BF16),
         pltpu.VMEM((2, 4, 16, D), BF16),
         pltpu.VMEM((2, 4, 16, D), BF16),
+        pltpu.VMEM((16, D), F32),
         pltpu.VMEM((2, 16, D), BF16),
         pltpu.VMEM((4, 4, 4, ROWS, WIDE), BF16),
         pltpu.VMEM((4, 3, 4, ROWS, WIDE), BF16),
@@ -412,25 +494,26 @@
         pltpu.VMEM((8, 2, D), F32),
         pltpu.VMEM((16, 2, D), F32),
         pltpu.VMEM((2, D), F32),
+        dma((8,)),
         dma((4, 15)), dma((4, 16)),
         dma((7,)), dma((8,)),
-        dma((2, 7)), dma((2, 8)),
-        dma((2, 5)), dma((2, 5)),
+        dma((2, 8)), dma((2, 8)),
+        dma((2,)), dma((2,)),
+        dma((2, 4)), dma((2, 4)),
+        dma((2, 4)), dma((2,)),
         dma((4, 6)), dma((4, 6)),
         dma((8,)), dma((8,)),
         dma((16,)), dma((16,)),
     ]
-    outs = pl.pallas_call(
+    grads, weight_grad, scales = pl.pallas_call(
         kernel,
         out_shape=(
             jax.ShapeDtypeStruct((2, 16, D), BF16),
-            shard,
-            shard,
-            shard,
+            jax.ShapeDtypeStruct((ROWS, 4 * WIDE), F32),
             jax.ShapeDtypeStruct((2, D), F32),
         ),
-        in_specs=[vmem] * 7,
-        out_specs=(vmem,) * 5,
+        in_specs=[vmem] * 4 + [pl.BlockSpec(memory_space=pl.ANY)],
+        out_specs=(vmem,) * 3,
         scratch_shapes=scratch,
         compiler_params=pltpu.CompilerParams(
             collective_id=0, has_side_effects=True, vmem_limit_bytes=56 * 1024 * 1024
@@ -438,14 +521,17 @@
         cost_estimate=pl.CostEstimate(flops=3 * 10**9, bytes_accessed=10**7, transcendentals=10**5),
     )(
         x_in.reshape(2, 16, D),
-        out_grad.reshape(2, 8, 16, D),
+        out_grad.reshape(2, 128, D).transpose(0, 2, 1),
         layer_scale,
         norm_gain,
-        master[0],
-        moment_one[0],
-        moment_two[0],
+        master.reshape(ROWS, 8, 128),
     )
-    grads, new_master, first, second, scales = outs
+    bias_one = 1.0 - beta_one**adam_step
+    bias_two = 1.0 - beta_two**adam_step
+    first = beta_one * moment_one[0] + (1.0 - beta_one) * weight_grad
+    second = beta_two * moment_two[0] + (1.0 - beta_two) * weight_grad * weight_grad
+    update = first / bias_one / (jnp.sqrt(second / bias_two) + adam_eps)
+    new_master = master[0] - learn_rate * (update + weight_decay * master[0])
     return (grads.reshape(1, 2, 1, 16, D), new_master[None], first[None], second[None], scales[None])
 
 

time: 182 us -> 171 us (0.940)
  the two profiles are of different devices: /device:TPU:64 before, /device:TPU:1 now
where the time goes in v3:
time: 171 us; the launch traced here: 170 us
  Pallas kernels  163 us (95%)
  local copies, waits for them, and re-layouts  4.84 us (3%)
    pallas_call x1, Pallas kernels, local(): pl.pallas_call(kernel, out_shape=(jax.ShapeDtypeStruct((2, 16, D), BF16),...  163 us
    unnamed x15, local copies, waits for them, and re-layouts  4.84 us

profile of v3, /device:TPU:1, one launch (start us, length us, event | category | flops | bytes accessed | tf_op | source)
XLA Modules:
  0.0 170.3 jit_solution(17460297731380710044)
XLA Ops:
  0.6 0.0 copy-start
  0.6 0.0 copy-start.1
  0.7 0.0 copy-start.2
  0.7 163.3 %shard_map.110 = (bf16[2,16,1600]{2,1,0:T(8,128)(2,1)}, f32[100,1024]{1,0:T(8,128)}, f32[2,1600]{1,0:T(2,128)}) custom-call(bf16[2,16,1600]{2,1,0:T(8,128)(2,1)} %bitcast.42, bf16[2,1600,128]{2,1,0:T(8,128)(2,1)} %bitcast.41, f32[1,1600]{1,0:T(1,128)} %ls_ref.1, f32[1,1600]{1,0:T(1,128)} %gain_ref.1, f32[100,8,128]{2,1,0:T(8,128)} %bitcast.38), custom_call_target="tpu_custom_call" | custom-call | flops 3000000000 | bytes 10000000 | tf_op jit(solution)/shard_map/pallas_call | solution.py:508
  164.0 0.0 copy-done
  164.0 0.0 copy-done.1
  164.0 0.0 copy-done.2
  164.0 1.4 fusion.5
  165.5 1.2 copy.17
  166.7 1.2 copy.15
  167.8 0.0 copy-start.3
  167.8 1.2 copy.16
  169.0 0.0 copy-done.3
  169.0 0.0 copy-start.4
  169.0 0.6 copy.36
  169.6 0.1 copy-done.4
  169.7 0.6 copy.37
Async XLA Ops:
  0.6 163.4 %copy-start = (f32[1,100,1024]{2,0,1:T(1,128)S(1)}, f32[1,100,1024]{2,0,1:T(1,128)}, u32[]{:S(2)}) copy-start(f32[1,100,1024]{2,0,1:T(1,128)} %param.11) | copy-start | bytes 1228804
  0.6 163.4 %copy-start.1 = (f32[1,100,1024]{2,0,1:T(1,128)S(1)}, f32[1,100,1024]{2,0,1:T(1,128)}, u32[]{:S(2)}) copy-start(f32[1,100,1024]{2,0,1:T(1,128)} %param.13) | copy-start | bytes 1228804
  0.7 163.4 %copy-start.2 = (f32[1,100,1024]{2,0,1:T(1,128)S(1)}, f32[1,100,1024]{2,0,1:T(1,128)}, u32[]{:S(2)}) copy-start(f32[1,100,1024]{2,0,1:T(1,128)} %param.12) | copy-start | bytes 1228804
  167.8 1.2 copy-start.3
  169.0 0.7 copy-start.4

commit v4 on v3

--- a/solution.py
+++ b/solution.py
@@ -9,6 +9,7 @@
 from jax.sharding import PartitionSpec as P
 
 HD = 128
+LEFT = 896
 D = 1600
 ROWS = 100
 WIDE = 256
@@ -34,8 +35,8 @@
 def kernel(
     x_ref, og_ref, ls_ref, gain_ref, master_ref,
     ig_ref, grad_ref, sg_ref,
-    wload, wland, dense, wide, xall, normed, flat, qkv, probs, att, inc, scaled, dproj,
-    part, s1land, arrived, passing, running, own_out, gsend, gland1, gmid, gmid_send, gland2, small, sm_t, sm_d, sm_send,
+    wload, wland, dense, wide, xall, normed, flat, qkv, probs, att, inc_l, inc_r, scaled, dproj,
+    part, s1land, arrived_l, arrived_r, passing_l, passing_r, passing, running, own_out, gsend, gland1, gmid, gmid_send, gland2, small, sm_t, sm_d, sm_send,
     m_s, w_ss, w_rs, x_ss, x_rs, a_ss, a_rs, c_ss, c_rs, r_ss, r_rs, o_ss, o_rs, g_ss, g_rs, t_ss, t_rs, d_ss, d_rs,
 ):
     p = lax.axis_index("pipe")
@@ -82,7 +83,7 @@
     for q in range(4):
         loads[2 * q].wait()
         loads[2 * q + 1].wait()
-        wland[q, r] = jnp.concatenate([wload[2 * q], wload[2 * q + 1]], axis=1).astype(BF16)
+        wland[q // 2, r, q % 2] = jnp.concatenate([wload[2 * q], wload[2 * q + 1]], axis=1).astype(BF16)
     pl.semaphore_wait(barrier, 24)
 
     def at(h, near, far):
@@ -114,54 +115,50 @@
 
     pending = []
 
-    def wsend(q, s, slot, where):
-        pending.append(send(wland.at[q, s], wland.at[q, s], w_ss.at[q, slot], w_rs.at[q, s], {"dp": where}))
+    def wpair(h, s, slot, where):
+        pending.append(send(wland.at[h, s], wland.at[h, s], w_ss.at[h, slot], w_rs.at[h, s, 0], {"dp": where}))
+
+    def wone(h, s, i, slot, where):
+        pending.append(send(wland.at[h, s, i], wland.at[h, s, i], w_ss.at[h, slot], w_rs.at[h, s, i], {"dp": where}))
 
     for h in range(2):
         near, far = coords(h)
-        for q in (2 * h, 2 * h + 1):
-            wsend(q, r, 0, at(h, up(near, 1), far))
-            wsend(q, r, 1, at(h, up(near, 3), far))
+        wpair(h, r, 0, at(h, up(near, 1), far))
+        wpair(h, r, 1, at(h, up(near, 3), far))
     xall[t] = x_ref[...]
     x_copies = spread(xall, x_ss, x_rs)
     for h in range(2):
         near, far = coords(h)
-        for q in (2 * h, 2 * h + 1):
-            wsend(q, r, 3, at(h, near, up(far, 1)))
-            wsend(q, r, 4, at(h, near, up(far, 3)))
+        wpair(h, r, 4, at(h, near, up(far, 1)))
+        wpair(h, r, 5, at(h, near, up(far, 3)))
     for h in range(2):
         near, far = coords(h)
-        for q in (2 * h, 2 * h + 1):
-            below = at(h, up(near, 3), far)
-            above = at(h, up(near, 1), far)
-            landed(wland.at[q, below], w_rs.at[q, below])
-            if q % 2 == 0:
-                wsend(q, below, 2, above)
-            landed(wland.at[q, above], w_rs.at[q, above])
-            if q % 2 == 1:
-                wsend(q, above, 2, below)
-            for j, s in ((1, below), (2, above)):
-                wsend(q, s, 3 + 3 * j, at(h, near, up(far, 1)))
-                wsend(q, s, 4 + 3 * j, at(h, near, up(far, 3)))
+        below = at(h, up(near, 3), far)
+        above = at(h, up(near, 1), far)
+        landed(wland.at[h, below], w_rs.at[h, below, 0])
+        wone(h, below, 0, 2, above)
+        landed(wland.at[h, above], w_rs.at[h, above, 0])
+        wone(h, above, 1, 3, below)
+        for j, s in ((1, below), (2, above)):
+            wpair(h, s, 4 + 4 * j, at(h, near, up(far, 1)))
+            wpair(h, s, 5 + 4 * j, at(h, near, up(far, 3)))
     for h in range(2):
         near, far = coords(h)
-        for q in (2 * h, 2 * h + 1):
-            s = at(h, up(near, 2), far)
-            landed(wland.at[q, s], w_rs.at[q, s])
-            wsend(q, s, 12, at(h, near, up(far, 1)))
-            wsend(q, s, 13, at(h, near, up(far, 3)))
+        s = at(h, up(near, 2), far)
+        for i in range(2):
+            landed(wland.at[h, s, i], w_rs.at[h, s, i])
+        wpair(h, s, 16, at(h, near, up(far, 1)))
+        wpair(h, s, 17, at(h, near, up(far, 3)))
+
     for j, step in enumerate((0, 3, 1, 2)):
         for h in range(2):
             near, far = coords(h)
-            for q in (2 * h, 2 * h + 1):
-                lower = at(h, up(near, step), up(far, 3))
-                upper = at(h, up(near, step), up(far, 1))
-                landed(wland.at[q, lower], w_rs.at[q, lower])
-                if q % 2 == 0:
-                    wsend(q, lower, 5 + 3 * j, at(h, near, up(far, 1)))
-                landed(wland.at[q, upper], w_rs.at[q, upper])
-                if q % 2 == 1:
-                    wsend(q, upper, 5 + 3 * j, at(h, near, up(far, 3)))
+            lower = at(h, up(near, step), up(far, 3))
+            upper = at(h, up(near, step), up(far, 1))
+            landed(wland.at[h, lower], w_rs.at[h, lower, 0])
+            wone(h, lower, 0, 6 + 4 * j, at(h, near, up(far, 1)))
+            landed(wland.at[h, upper], w_rs.at[h, upper, 0])
+            wone(h, upper, 1, 7 + 4 * j, at(h, near, up(far, 3)))
     x_copies += relay(xall, x_ss, x_rs)
     settle(xall, x_rs)
 
@@ -174,20 +171,22 @@
     @pl.when(p == 3)
     def _():
         for m in range(2):
-            inc[m] = og_ref[m].T.reshape(8, 16, D)
+            rows = og_ref[m].T.reshape(8, 16, D)
+            inc_l[m] = rows[:, :, :LEFT]
+            inc_r[m] = rows[:, :, LEFT:]
 
     flat[...] = normed[...].T
 
     for h in range(2):
         near, far = coords(h)
-        for q in (2 * h, 2 * h + 1):
-            for step in range(4):
-                s = at(h, up(near, step), up(far, 2))
-                landed(wland.at[q, s], w_rs.at[q, s])
+        for step in (0, 3, 1, 2):
+            s = at(h, up(near, step), up(far, 2))
+            for i in range(2):
+                landed(wland.at[h, s, i], w_rs.at[h, s, i])
 
     for q in range(4):
         for s in range(16):
-            wide[s * ROWS : (s + 1) * ROWS] = wland[q, s].astype(F32)
+            wide[s * ROWS : (s + 1) * ROWS] = wland[q // 2, s, q % 2].astype(F32)
         dense[q] = wide[...].astype(BF16)
         if q < 3:
             qkv[q] = dot(normed[...], dense[q], (1, 0)).astype(BF16)
@@ -201,9 +200,14 @@
             probs[m, head] = prob
             att[row, col] = dot(prob.astype(BF16), qkv[2, row, col], (1, 0)).astype(BF16)
 
+    inc, arrived, parting = (inc_l, inc_r), (arrived_l, arrived_r), (passing_l, passing_r)
+
+    def incoming(m):
+        return jnp.concatenate([inc_l[m].reshape(128, LEFT), inc_r[m].reshape(128, D - LEFT)], axis=1).astype(F32)
+
     def backward(m):
         row = slice(m * 128, (m + 1) * 128)
-        scaled_now = (ls_ref[...] * inc[m].reshape(128, D).astype(F32)).astype(BF16)
+        scaled_now = (ls_ref[...] * incoming(m)).astype(BF16)
         scaled[row] = scaled_now
         d_att = dot(scaled_now, dense[3], (1, 0)).astype(BF16)
         for head in range(2):
@@ -226,7 +230,7 @@
     def scale_part(m):
         row = slice(m * 128, (m + 1) * 128)
         out_rows = dot(att[row], dense[3], (1, 1))
-        return jnp.sum(inc[m].reshape(128, D).astype(F32) * out_rows, axis=0, keepdims=True)
+        return jnp.sum(incoming(m) * out_rows, axis=0, keepdims=True)
 
     def remote(src, dst, ss, rs, to):
         return pltpu.make_async_remote_copy(
@@ -239,51 +243,56 @@
     def first_stage(m):
         return remote(part.at[m, 1 - core], s1land.at[m], c_ss.at[m], c_rs.at[m], {"tensor": partner})
 
-    def across(m, j):
+    def across(m, j, c):
+        ref = inc[c].at[m, 2 * j + core]
+        return remote(ref, ref, a_ss.at[m, c, j], a_rs.at[m, c, 2 * j + core], {"tensor": partner})
+
+    def down(m, j, c):
+        ref = inc[c].at[m, 2 * j + core]
+        return remote(ref, ref, a_ss.at[m, c, 4 + j], a_rs.at[m, c, 2 * j + core], below)
+
+    def sum_down(m, j, c):
+        return remote(parting[c].at[m, j], arrived[c].at[m, j], r_ss.at[m, c, j], r_rs.at[m, c, j], below)
+
+    def hand_on(m, j, c):
         i = 2 * j + core
-        return remote(inc.at[m, i], inc.at[m, i], a_ss.at[m, j], a_rs.at[m, i], {"tensor": partner})
-
-    def down(m, j):
-        i = 2 * j + core
-        return remote(inc.at[m, i], inc.at[m, i], a_ss.at[m, 4 + j], a_rs.at[m, i], below)
-
-    def sum_down(m, j):
-        return remote(passing.at[m, j], arrived.at[m, j], r_ss.at[m, j], r_rs.at[m, j], below)
-
-    def hand_on(m, j):
-        return remote(passing.at[m, j], inc.at[m, 2 * j + core], r_ss.at[m, j], a_rs.at[m, 2 * j + core], section_below)
+        return remote(parting[c].at[m, j], inc[c].at[m, i], r_ss.at[m, c, j], a_rs.at[m, c, i], section_below)
 
     def give_back(m, j):
         return remote(passing.at[m, j], own_out.at[m], o_ss.at[m, j], o_rs.at[m], {"tensor": 2 * j + core})
 
     def take_piece(m, j):
-        landed(inc.at[m, 2 * j + core], a_rs.at[m, 2 * j + core])
-
-        @pl.when(chip > 0)
-        def _():
-            down(m, j).start()
-
-        across(m, j).start()
+        for c in range(2):
+            landed(inc[c].at[m, 2 * j + core], a_rs.at[m, c, 2 * j + core])
+
+            @pl.when(chip > 0)
+            def _():
+                down(m, j, c).start()
+
+            across(m, j, c).start()
 
     def take_rest(m):
         for j in range(4):
-            landed(inc.at[m, 2 * j + 1 - core], a_rs.at[m, 2 * j + 1 - core])
+            for c in range(2):
+                landed(inc[c].at[m, 2 * j + 1 - core], a_rs.at[m, c, 2 * j + 1 - core])
 
     def reduce_start(m):
         landed(s1land.at[m], c_rs.at[m])
 
     def reduce_piece(m, j):
-        running[...] = part[m, core, j].astype(F32) + s1land[m, j].astype(F32)
-
-        @pl.when(chip < 3)
-        def _():
-            landed(arrived.at[m, j], r_rs.at[m, j])
-            running[...] += arrived[m, j].astype(F32)
-
-        @pl.when(chip > 0)
-        def _():
-            passing[m, j] = running[...].astype(BF16)
-            sum_down(m, j).start()
+        for c, cols in enumerate((slice(0, LEFT), slice(LEFT, D))):
+            own = part[m, core, j, :, cols].astype(F32) + s1land[m, j, :, cols].astype(F32)
+            running[:, cols] = own
+
+            @pl.when(chip < 3)
+            def _():
+                landed(arrived[c].at[m, j], r_rs.at[m, c, j])
+                running[:, cols] = own + arrived[c][m, j].astype(F32)
+
+            @pl.when(chip > 0)
+            def _():
+                parting[c][m, j] = running[:, cols].astype(BF16)
+                sum_down(m, j, c).start()
 
         @pl.when(chip == 0)
         def _():
@@ -294,12 +303,17 @@
             unit = rows * inverse
             e = total * gain
             d_input = inverse * (e - unit * jnp.mean(e * unit, axis=-1, keepdims=True))
-            passing[m, j] = (inc[m, i].astype(F32) + d_input).astype(BF16)
+            held = jnp.concatenate([inc_l[m, i], inc_r[m, i]], axis=1)
+            passed = (held.astype(F32) + d_input).astype(BF16)
+            passing_l[m, j] = passed[:, :LEFT]
+            passing_r[m, j] = passed[:, LEFT:]
 
             @pl.when(p > 0)
             def _():
-                hand_on(m, j).start()
-
+                for c in range(2):
+                    hand_on(m, j, c).start()
+
+            passing[m, j] = passed
             if j > 0:
                 give_back(m, j).start()
             small[1:2] += jnp.sum(total * unit, axis=0, keepdims=True)
@@ -437,16 +451,20 @@
         @pl.when(p < 3)
         def _():
             for j in range(4):
-                across(m, j).wait_send()
-
-                @pl.when(chip > 0)
-                def _():
-                    down(m, j).wait_send()
+                for c in range(2):
+                    across(m, j, c).wait_send()
+
+            @pl.when(chip > 0)
+            def _():
+                for j in range(4):
+                    for c in range(2):
+                        down(m, j, c).wait_send()
 
         @pl.when(chip > 0)
         def _():
             for j in range(4):
-                sum_down(m, j).wait_send()
+                for c in range(2):
+                    sum_down(m, j, c).wait_send()
             landed(own_out.at[m], o_rs.at[m])
             ig_ref[m] = own_out[m]
 
@@ -459,7 +477,8 @@
             @pl.when(p > 0)
             def _():
                 for j in range(4):
-                    hand_on(m, j).wait_send()
+                    for c in range(2):
+                        hand_on(m, j, c).wait_send()
 
 
 def local(x_in, out_grad, layer_scale, norm_gain, master, moment_one, moment_two):
@@ -467,7 +486,7 @@
     dma = pltpu.SemaphoreType.DMA
     scratch = [
         pltpu.VMEM((8, ROWS, 128), F32),
-        pltpu.VMEM((4, 16, ROWS, WIDE), BF16),
+        pltpu.VMEM((2, 16, 2, ROWS, WIDE), BF16),
         pltpu.VMEM((4, D, WIDE), BF16),
         pltpu.VMEM((D, WIDE), F32),
         pltpu.VMEM((8, 2, 16, D), BF16),
@@ -476,12 +495,16 @@
         pltpu.VMEM((3, 256, WIDE), BF16),
         pltpu.VMEM((2, 2, 128, 128), F32),
         pltpu.VMEM((256, WIDE), BF16),
-        pltpu.VMEM((2, 8, 16, D), BF16),
+        pltpu.VMEM((2, 8, 16, LEFT), BF16),
+        pltpu.VMEM((2, 8, 16, D - LEFT), BF16),
         pltpu.VMEM((256, D), BF16),
         pltpu.VMEM((3, 256, WIDE), BF16),
         pltpu.VMEM((2, 2, 4, 16, D), BF16),
         pltpu.VMEM((2, 4, 16, D), BF16),
-        pltpu.VMEM((2, 4, 16, D), BF16),
+        pltpu.VMEM((2, 4, 16, LEFT), BF16),
+        pltpu.VMEM((2, 4, 16, D - LEFT), BF16),
+        pltpu.VMEM((2, 4, 16, LEFT), BF16),
+        pltpu.VMEM((2, 4, 16, D - LEFT), BF16),
         pltpu.VMEM((2, 4, 16, D), BF16),
         pltpu.VMEM((16, D), F32),
         pltpu.VMEM((2, 16, D), BF16),
@@ -495,11 +518,11 @@
         pltpu.VMEM((16, 2, D), F32),
         pltpu.VMEM((2, D), F32),
         dma((8,)),
-        dma((4, 15)), dma((4, 16)),
+        dma((2, 20)), dma((2, 16, 2)),
         dma((7,)), dma((8,)),
-        dma((2, 8)), dma((2, 8)),
+        dma((2, 2, 8)), dma((2, 2, 8)),
         dma((2,)), dma((2,)),
-        dma((2, 4)), dma((2, 4)),
+        dma((2, 2, 4)), dma((2, 2, 4)),
         dma((2, 4)), dma((2,)),
         dma((4, 6)), dma((4, 6)),
         dma((8,)), dma((8,)),

time: 171 us -> 167 us (0.977)
  Pallas kernels: 163 us -> 160 us
    pallas_call x1, Pallas kernels: 163 us -> 160 us  [local(): pl.pallas_call(kernel, out_shape=(jax.ShapeDtypeStruct((2, 16, D), BF16),...]
where the time goes in v4:
time: 167 us
  Pallas kernels  160 us (96%)
  local copies, waits for them, and re-layouts  4.84 us (3%)
    pallas_call x1, Pallas kernels, local(): pl.pallas_call(kernel, out_shape=(jax.ShapeDtypeStruct((2, 16, D), BF16),...  160 us
    unnamed x15, local copies, waits for them, and re-layouts  4.84 us

profile of v4, /device:TPU:1, one launch (start us, length us, event | category | flops | bytes accessed | tf_op | source)
XLA Modules:
  0.0 166.7 jit_solution(13495949494961017881)
XLA Ops:
  0.6 0.0 copy-start
  0.6 0.0 copy-start.1
  0.7 0.0 copy-start.2
  0.7 159.7 %shard_map.110 = (bf16[2,16,1600]{2,1,0:T(8,128)(2,1)}, f32[100,1024]{1,0:T(8,128)}, f32[2,1600]{1,0:T(2,128)}) custom-call(bf16[2,16,1600]{2,1,0:T(8,128)(2,1)} %bitcast.42, bf16[2,1600,128]{2,1,0:T(8,128)(2,1)} %bitcast.41, f32[1,1600]{1,0:T(1,128)} %ls_ref.1, f32[1,1600]{1,0:T(1,128)} %gain_ref.1, f32[100,8,128]{2,1,0:T(8,128)} %bitcast.38), custom_call_target="tpu_custom_call" | custom-call | flops 3000000000 | bytes 10000000 | tf_op jit(solution)/shard_map/pallas_call | solution.py:531
  160.4 0.0 copy-done
  160.4 0.0 copy-done.1
  160.4 0.0 copy-done.2
  160.4 1.4 fusion.5
  161.9 1.2 copy.17
  163.0 1.2 copy.15
  164.2 0.0 copy-start.3
  164.2 1.2 copy.16
  165.4 0.0 copy-done.3
  165.4 0.0 copy-start.4
  165.4 0.6 copy.36
  166.0 0.1 copy-done.4
  166.1 0.6 copy.37
Async XLA Ops:
  0.6 159.8 %copy-start = (f32[1,100,1024]{2,0,1:T(1,128)S(1)}, f32[1,100,1024]{2,0,1:T(1,128)}, u32[]{:S(2)}) copy-start(f32[1,100,1024]{2,0,1:T(1,128)} %param.11) | copy-start | bytes 1228804
  0.6 159.8 %copy-start.1 = (f32[1,100,1024]{2,0,1:T(1,128)S(1)}, f32[1,100,1024]{2,0,1:T(1,128)}, u32[]{:S(2)}) copy-start(f32[1,100,1024]{2,0,1:T(1,128)} %param.13) | copy-start | bytes 1228804
  0.7 159.8 %copy-start.2 = (f32[1,100,1024]{2,0,1:T(1,128)S(1)}, f32[1,100,1024]{2,0,1:T(1,128)}, u32[]{:S(2)}) copy-start(f32[1,100,1024]{2,0,1:T(1,128)} %param.12) | copy-start | bytes 1228804
  164.2 1.2 copy-start.3
  165.4 0.7 copy-start.4

commit v5 on v4

--- a/solution.py
+++ b/solution.py
@@ -334,6 +334,16 @@
             device_id={"dp": to}, device_id_type=MESH,
         )
 
+    def gsum(q, k):
+        near, far = coords(q // 2)
+        ahead, back = (1, 3) if q % 2 == 0 else (3, 1)
+        place, slot = up(near, (2, back, ahead, 0)[k]), (2, 6, 7, 8)[k]
+        return place, pltpu.make_async_remote_copy(
+            src_ref=gsend.at[q, up(far, ahead), place], dst_ref=gland1.at[q, 2, place],
+            send_sem=g_ss.at[q, slot], recv_sem=g_rs.at[q, slot],
+            device_id={"dp": at(q // 2, near, up(far, ahead))}, device_id_type=MESH,
+        )
+
     order = (3, 0, 1, 2)
 
     def weight_grads():
@@ -396,8 +406,10 @@
         near, far = coords(q // 2)
         line = up(far, 1 if q % 2 == 0 else 3)
         landed(gland1.at[q, 0], g_rs.at[q, 0])
-        gsend[q, line] = (gsend[q, line].astype(F32) + gland1[q, 0].astype(F32)).astype(BF16)
-        gcopy(q, 2, False).start()
+        for k in range(4):
+            place, copy = gsum(q, k)
+            gsend[q, line, place] = (gsend[q, line, place].astype(F32) + gland1[q, 0, place].astype(F32)).astype(BF16)
+            copy.start()
 
     total = small[...]
     for k in range(1, 8):
@@ -409,27 +421,33 @@
         other = lax.rem(r + k, 16)
         pending.append(send(sm_send, sm_d.at[r], d_ss.at[k], d_rs.at[r], {"dp": other}))
 
-    for q in order:
-        near, far = coords(q // 2)
-        landed(gland1.at[q, 1], g_rs.at[q, 1])
-        landed(gland1.at[q, 2], g_rs.at[q, 2])
-        gmid[q] = gsend[q, far].astype(F32) + gland1[q, 1].astype(F32) + gland1[q, 2].astype(F32)
-        gmid_send[q] = gmid[q].astype(BF16)
-        gcopy(q, 0, True).start()
-        gcopy(q, 1, True).start()
-    for q in order:
-        near, far = coords(q // 2)
-        line = up(near, 1 if q % 2 == 0 else 3)
-        landed(gland2.at[q, 0], g_rs.at[q, 3])
-        gmid_send[q, line] = (gmid[q, line] + gland2[q, 0].astype(F32)).astype(BF16)
-        gcopy(q, 2, True).start()
+    for k in range(4):
+        for q in order:
+            near, far = coords(q // 2)
+            if k == 0:
+                landed(gland1.at[q, 1], g_rs.at[q, 1])
+            place, copy = gsum(q, k)
+            copy.wait_recv()
+            chunk = gsend[q, far, place].astype(F32) + gland1[q, 1, place].astype(F32) + gland1[q, 2, place].astype(F32)
+            if k < 2:
+                gmid_send[q, place] = chunk.astype(BF16)
+                gcopy(q, k, True).start()
+            elif k == 2:
+                landed(gland2.at[q, 0], g_rs.at[q, 3])
+                gmid_send[q, place] = (chunk + gland2[q, 0].astype(F32)).astype(BF16)
+                gcopy(q, 2, True).start()
+            else:
+                gmid[q] = chunk
+    stores = []
     for q in order:
         near, far = coords(q // 2)
         landed(gland2.at[q, 1], g_rs.at[q, 4])
         landed(gland2.at[q, 2], g_rs.at[q, 5])
-        grad_ref[:, q * WIDE : (q + 1) * WIDE] = (
-            gmid[q, near] + gland2[q, 1].astype(F32) + gland2[q, 2].astype(F32)
-        )
+        grad = gmid[q] + gland2[q, 1].astype(F32) + gland2[q, 2].astype(F32)
+        for b in (2 * q, 2 * q + 1):
+            wload[b] = grad[:, (b % 2) * 128 : (b % 2 + 1) * 128]
+            stores.append(pltpu.make_async_copy(wload.at[b], grad_ref.at[:, b], m_s.at[b]))
+            stores[-1].start()
 
     total = sm_send[...]
     for k in range(1, 16):
@@ -438,12 +456,17 @@
         total += sm_d[other]
     sg_ref[...] = total
 
+    for copy in stores:
+        copy.wait()
     for copy in pending + x_copies:
         copy.wait_send()
     for q in order:
         for kind in range(3):
+            gcopy(q, kind, True).wait_send()
+        for kind in range(2):
             gcopy(q, kind, False).wait_send()
-            gcopy(q, kind, True).wait_send()
+        for k in range(4):
+            gsum(q, k)[1].wait_send()
 
     for m in range(2):
         first_stage(m).wait_send()
@@ -510,7 +533,7 @@
         pltpu.VMEM((2, 16, D), BF16),
         pltpu.VMEM((4, 4, 4, ROWS, WIDE), BF16),
         pltpu.VMEM((4, 3, 4, ROWS, WIDE), BF16),
-        pltpu.VMEM((4, 4, ROWS, WIDE), F32),
+        pltpu.VMEM((4, ROWS, WIDE), F32),
         pltpu.VMEM((4, 4, ROWS, WIDE), BF16),
         pltpu.VMEM((4, 3, ROWS, WIDE), BF16),
         pltpu.VMEM((2, D), F32),
@@ -524,7 +547,7 @@
         dma((2,)), dma((2,)),
         dma((2, 2, 4)), dma((2, 2, 4)),
         dma((2, 4)), dma((2,)),
-        dma((4, 6)), dma((4, 6)),
+        dma((4, 9)), dma((4, 9)),
         dma((8,)), dma((8,)),
         dma((16,)), dma((16,)),
     ]
@@ -532,11 +555,11 @@
         kernel,
         out_shape=(
             jax.ShapeDtypeStruct((2, 16, D), BF16),
-            jax.ShapeDtypeStruct((ROWS, 4 * WIDE), F32),
+            jax.ShapeDtypeStruct((ROWS, 8, 128), F32),
             jax.ShapeDtypeStruct((2, D), F32),
         ),
         in_specs=[vmem] * 4 + [pl.BlockSpec(memory_space=pl.ANY)],
-        out_specs=(vmem,) * 3,
+        out_specs=(vmem, pl.BlockSpec(memory_space=pl.ANY), vmem),
         scratch_shapes=scratch,
         compiler_params=pltpu.CompilerParams(
             collective_id=0, has_side_effects=True, vmem_limit_bytes=56 * 1024 * 1024
@@ -551,11 +574,21 @@
     )
     bias_one = 1.0 - beta_one**adam_step
     bias_two = 1.0 - beta_two**adam_step
-    first = beta_one * moment_one[0] + (1.0 - beta_one) * weight_grad
-    second = beta_two * moment_two[0] + (1.0 - beta_two) * weight_grad * weight_grad
+    lines = (ROWS, 8, 128)
+    old, one, two = master.reshape(lines), moment_one.reshape(lines), moment_two.reshape(lines)
+    old, one, two, weight_grad = lax.optimization_barrier((old, one, two, weight_grad))
+    first = beta_one * one + (1.0 - beta_one) * weight_grad
+    second = beta_two * two + (1.0 - beta_two) * weight_grad * weight_grad
     update = first / bias_one / (jnp.sqrt(second / bias_two) + adam_eps)
-    new_master = master[0] - learn_rate * (update + weight_decay * master[0])
-    return (grads.reshape(1, 2, 1, 16, D), new_master[None], first[None], second[None], scales[None])
+    new_master = old - learn_rate * (update + weight_decay * old)
+    shape = master.shape
+    return (
+        grads.reshape(1, 2, 1, 16, D),
+        new_master.reshape(shape),
+        first.reshape(shape),
+        second.reshape(shape),
+        scales[None],
+    )
 
 
 def solution(mesh):

time: 167 us -> 165 us (0.988)
  local copies, waits for them, and re-layouts: 4.84 us -> 1.33 us
    unnamed x15 -> x12, local copies, waits for them, and re-layouts: 4.84 us -> 1.33 us
    sub x0 -> x1, other arithmetic: none -> 2.24 us  [local(): new_master = old - learn_rate * (update + weight_decay * old)]
where the time goes in v5:
time: 165 us
  Pallas kernels  160 us (97%)
  other arithmetic  2.24 us (1%)
    pallas_call x1, Pallas kernels, local(): pl.pallas_call(kernel, out_shape=(jax.ShapeDtypeStruct((2, 16, D), BF16),...  160 us

profile of v5, /device:TPU:1, one launch (start us, length us, event | category | flops | bytes accessed | tf_op | source)
XLA Modules:
  0.0 164.7 jit_solution(7547012604112784578)
XLA Ops:
  0.6 0.0 copy-start
  0.6 0.0 copy-start.1
  0.7 0.0 copy-start.2
  0.7 160.4 %shard_map.110 = (bf16[2,16,1600]{2,1,0:T(8,128)(2,1)}, f32[100,8,128]{2,1,0:T(8,128)}, f32[2,1600]{1,0:T(2,128)}) custom-call(bf16[2,16,1600]{2,1,0:T(8,128)(2,1)} %bitcast.24, bf16[2,1600,128]{2,1,0:T(8,128)(2,1)} %bitcast.23, f32[1,1600]{1,0:T(1,128)} %ls_ref.1, f32[1,1600]{1,0:T(1,128)} %gain_ref.1, f32[100,8,128]{2,1,0:T(8,128)} %bitcast.14), custom_call_target="tpu_custom_call" | custom-call | flops 3000000000 | bytes 10000000 | tf_op jit(solution)/shard_map/pallas_call | solution.py:554
  161.1 0.0 copy-done
  161.1 0.0 copy-done.1
  161.1 0.0 copy-done.2
  161.1 0.0 copy-start.3
  161.1 2.2 %multiply_subtract_fusion = (f32[100,8,128]{2,1,0:T(8,128)}, f32[100,8,128]{2,1,0:T(8,128)}, f32[100,8,128]{2,1,0:T(8,128)}) fusion(f32[100,8,128]{2,1,0:T(8,128)S(1)} %bitcast.15, f32[100,8,128]{2,1,0:T(8,128)} %get-tuple-element.16, f32[100,8,128]{2,1,0:T(8,128)S(1)} %bitcast.16, f32[100,8,128]{2,1,0:T(8,128)S(1)} %bitcast.17), kind=kLoop, calls=%fused_computation.2 | loop fusion | flops 1536000 | bytes 2867200 | tf_op jit(solution)/shard_map/sub | solution.py:583
  163.4 0.0 copy-done.3
  163.4 0.0 copy-start.4
  163.4 0.6 copy.22
  164.0 0.1 copy-done.4
  164.1 0.6 copy.23
Async XLA Ops:
  0.6 160.4 %copy-start = (f32[1,100,1024]{2,0,1:T(1,128)S(1)}, f32[1,100,1024]{2,0,1:T(1,128)}, u32[]{:S(2)}) copy-start(f32[1,100,1024]{2,0,1:T(1,128)} %param.11) | copy-start | bytes 1228804
  0.6 160.4 %copy-start.1 = (f32[1,100,1024]{2,0,1:T(1,128)S(1)}, f32[1,100,1024]{2,0,1:T(1,128)}, u32[]{:S(2)}) copy-start(f32[1,100,1024]{2,0,1:T(1,128)} %param.12) | copy-start | bytes 1228804
  0.7 160.4 %copy-start.2 = (f32[1,100,1024]{2,0,1:T(1,128)S(1)}, f32[1,100,1024]{2,0,1:T(1,128)}, u32[]{:S(2)}) copy-start(f32[1,100,1024]{2,0,1:T(1,128)} %param.13) | copy-start | bytes 1228804
  161.1 2.3 %copy-start.3 = (bf16[2,16,1600]{2,1,0:T(8,128)(2,1)S(1)}, bf16[2,16,1600]{2,1,0:T(8,128)(2,1)}, u32[]{:S(2)}) copy-start(bf16[2,16,1600]{2,1,0:T(8,128)(2,1)} %get-tuple-element.12) | copy-start | bytes 307204
  163.4 0.7 copy-start.4

commit v6 on v5

--- a/solution.py
+++ b/solution.py
@@ -393,11 +393,6 @@
     for j in range(4):
         reduce_piece(1, j)
 
-    small[0:1] = scale_part(0) + scale_part(1)
-    for k in range(1, 8):
-        other = lax.rem(t + k, 8)
-        pending.append(send(small, sm_t.at[t], t_ss.at[k], t_rs.at[t], {"tensor": other}))
-
     @pl.when(p > 0)
     def _():
         weight_grads()
@@ -410,6 +405,11 @@
             place, copy = gsum(q, k)
             gsend[q, line, place] = (gsend[q, line, place].astype(F32) + gland1[q, 0, place].astype(F32)).astype(BF16)
             copy.start()
+
+    small[0:1] = scale_part(0) + scale_part(1)
+    for k in range(1, 8):
+        other = lax.rem(t + k, 8)
+        pending.append(send(small, sm_t.at[t], t_ss.at[k], t_rs.at[t], {"tensor": other}))
 
     total = small[...]
     for k in range(1, 8):

time: 165 us -> 164 us (level)
  no operation moved by 1% of the time
where the time goes in v6:
time: 164 us
  Pallas kernels  159 us (97%)
  other arithmetic  2.24 us (1%)
    pallas_call x1, Pallas kernels, local(): pl.pallas_call(kernel, out_shape=(jax.ShapeDtypeStruct((2, 16, D), BF16),...  159 us

profile of v6, /device:TPU:1, one launch (start us, length us, event | category | flops | bytes accessed | tf_op | source)
XLA Modules:
  0.0 163.5 jit_solution(7810618103157729589)
XLA Ops:
  0.6 0.0 copy-start
  0.6 0.0 copy-start.1
  0.7 0.0 copy-start.2
  0.7 159.2 %shard_map.110 = (bf16[2,16,1600]{2,1,0:T(8,128)(2,1)}, f32[100,8,128]{2,1,0:T(8,128)}, f32[2,1600]{1,0:T(2,128)}) custom-call(bf16[2,16,1600]{2,1,0:T(8,128)(2,1)} %bitcast.24, bf16[2,1600,128]{2,1,0:T(8,128)(2,1)} %bitcast.23, f32[1,1600]{1,0:T(1,128)} %ls_ref.1, f32[1,1600]{1,0:T(1,128)} %gain_ref.1, f32[100,8,128]{2,1,0:T(8,128)} %bitcast.14), custom_call_target="tpu_custom_call" | custom-call | flops 3000000000 | bytes 10000000 | tf_op jit(solution)/shard_map/pallas_call | solution.py:554
  159.9 0.0 copy-done
  159.9 0.0 copy-done.1
  159.9 0.0 copy-done.2
  160.0 0.0 copy-start.3
  160.0 2.2 %multiply_subtract_fusion = (f32[100,8,128]{2,1,0:T(8,128)}, f32[100,8,128]{2,1,0:T(8,128)}, f32[100,8,128]{2,1,0:T(8,128)}) fusion(f32[100,8,128]{2,1,0:T(8,128)S(1)} %bitcast.15, f32[100,8,128]{2,1,0:T(8,128)} %get-tuple-element.16, f32[100,8,128]{2,1,0:T(8,128)S(1)} %bitcast.16, f32[100,8,128]{2,1,0:T(8,128)S(1)} %bitcast.17), kind=kLoop, calls=%fused_computation.2 | loop fusion | flops 1536000 | bytes 2867200 | tf_op jit(solution)/shard_map/sub | solution.py:583
  162.2 0.0 copy-done.3
  162.2 0.0 copy-start.4
  162.2 0.6 copy.22
  162.9 0.1 copy-done.4
  162.9 0.6 copy.23
Async XLA Ops:
  0.6 159.3 %copy-start = (f32[1,100,1024]{2,0,1:T(1,128)S(1)}, f32[1,100,1024]{2,0,1:T(1,128)}, u32[]{:S(2)}) copy-start(f32[1,100,1024]{2,0,1:T(1,128)} %param.11) | copy-start | bytes 1228804
  0.6 159.3 %copy-start.1 = (f32[1,100,1024]{2,0,1:T(1,128)S(1)}, f32[1,100,1024]{2,0,1:T(1,128)}, u32[]{:S(2)}) copy-start(f32[1,100,1024]{2,0,1:T(1,128)} %param.12) | copy-start | bytes 1228804
  0.7 159.3 %copy-start.2 = (f32[1,100,1024]{2,0,1:T(1,128)S(1)}, f32[1,100,1024]{2,0,1:T(1,128)}, u32[]{:S(2)}) copy-start(f32[1,100,1024]{2,0,1:T(1,128)} %param.13) | copy-start | bytes 1228804
  160.0 2.3 %copy-start.3 = (bf16[2,16,1600]{2,1,0:T(8,128)(2,1)S(1)}, bf16[2,16,1600]{2,1,0:T(8,128)(2,1)}, u32[]{:S(2)}) copy-start(bf16[2,16,1600]{2,1,0:T(8,128)(2,1)} %get-tuple-element.12) | copy-start | bytes 307204
  162.2 0.7 copy-start.4
